TPU v7x, 128 devices: a whole 4x4x4 slice. The times are simulated.
128 devices in a mesh: lon: 16 (over z_lo, x, core), lat: 8 (over y, z_hi).
Axes of the slice: x: 4, y: 4, z: 4 (z_hi: 2, z_lo: 2; z = z_hi * 2 + z_lo), core: 2. Of those that a mesh axis runs over, the one named last changes fastest.
Arguments:
- fields: bfloat16 [192, 384, 3, 512], P('lat', 'lon'), may hold values from -6 to 6
- region_ids: int32 [192], P('lat'), may hold values from 0 to 31, never falling along the last dimension, each value on 1 to 12 neighbouring positions
- w_qkv: bfloat16 [1536, 512], P(('lon', 'lat')), may hold values from -2 to 2
- w_proj: bfloat16 [512, 512], P(('lon', 'lat')), may hold values from -0.25 to 0.25
- grad_output: bfloat16 [192, 384, 3, 512], P('lat', 'lon'), may hold values from -6 to 6
Outputs:
- block_out: bfloat16 [192, 384, 3, 512], P('lat', 'lon')
- grad_fields: bfloat16 [192, 384, 3, 512], P('lat', 'lon')
- grad_w_qkv: float32 [1536, 512], P(('lon', 'lat'))
- grad_w_proj: float32 [512, 512], P(('lon', 'lat'))
Inputs may be any that keep to these rules, and one draw needn't show every extreme that they name: `region_ids`: region ids never fall along the rows; each region spans 1 to 12 rows.
All inputs are finite; a program needn't handle non-finite values.
Results may differ from a plain program's by a relative error of at most 0.018.
The roundings to bfloat16 on the way count: a program that leaves them out, or rounds other values in their place, can miss the bound.
Values may be sent and summed in bfloat16 or wider, within the bound.
A program may use at most 128 MiB of HBM per device.

v0:
```python
import jax
import jax.numpy as jnp
from jax import lax
from jax.sharding import Mesh
from jax.sharding import PartitionSpec as P

HEADS = 8
HEAD = 64
WIN = 12
LON = ("lon_0", "lon_1", "lon_2")
LAT = ("lat_0", "lat_1")
LON_LAT = ("lon_0", "lon_1", "lon_2", "lat_0", "lat_1")


EPSILON = 1e-05


def shifted_2(block, axis, distance):
    devices = range(lax.axis_size(axis))
    route = [((i - distance) % len(devices), i) for i in devices]
    return lax.ppermute(block, axis, route)


def laid_out(pieces, dim):
    pieces = jnp.moveaxis(pieces, 0, dim)
    lengths = pieces.shape
    return pieces.reshape(*lengths[:dim], lengths[dim] * lengths[dim + 1], *lengths[dim + 2 :])


def gather_together(arrays, axis, dims):
    vector = jnp.concatenate([a.reshape(-1) for a in arrays])
    lines, at, outs = (lax.all_gather(vector, axis), 0, [])
    for a, dim in zip(arrays, dims):
        pieces = lines[:, at : at + a.size].reshape(-1, *a.shape)
        outs.append(laid_out(pieces, dim))
        at += a.size
    return tuple(outs)


def in_blocks(shard, dim, count):
    before, after = (shard.shape[:dim], shard.shape[dim + 1 :])
    return jnp.moveaxis(shard.reshape(*before, count, -1, *after), dim, 0)


def cut_rows(length, count):
    lap = length // count
    if lap >= 8:
        lap -= lap % 8
    return [lap * k for k in range(1, count)]


def own_block(pieces, axes, sequence):
    inside = pieces.shape[1:]
    pieces = pieces.reshape(*(lax.axis_size(a) for a in axes), *inside)
    pieces = jnp.moveaxis(pieces, sequence, range(len(axes))).reshape(-1, *inside)
    for k in sequence:
        pieces = lax.psum_scatter(pieces, axes[k], scatter_dimension=0, tiled=True)
    return pieces[0]


def spread_scatter(shard, axes, dim):
    pieces = in_blocks(shard, dim, lax.axis_size(axes))
    widest = max(range(1, max(2, pieces.ndim - 1)), key=lambda d: pieces.shape[d])
    count, outs = (len(axes), [])
    for first, slab in enumerate(
        jnp.split(pieces, cut_rows(pieces.shape[widest], count), axis=widest)
    ):
        if slab.size:
            sequence = [(first + k) % count for k in range(count)]
            outs.append(own_block(slab, axes, sequence))
    return jnp.concatenate(outs, axis=widest - 1)


def to_windows(grid, side):
    rows, cols, depth, width = grid.shape
    blocks = grid.reshape(rows // side, side, cols // side, side, depth, width)
    return blocks.transpose(0, 2, 1, 3, 4, 5).reshape(-1, side * side * depth, width)


def from_windows(windows, rows, cols, side):
    depth = windows.shape[1] // (side * side)
    width = windows.shape[2]
    blocks = windows.reshape(rows // side, cols // side, side, side, depth, width)
    return blocks.transpose(0, 2, 1, 3, 4, 5).reshape(rows, cols, depth, width)


def window_regions(region_ids, cols, depth, side):
    bands = region_ids.shape[0] // side
    spread = jnp.broadcast_to(
        region_ids.reshape(bands, 1, side, 1, 1), (bands, cols // side, side, side, depth)
    )
    return spread.reshape(bands * (cols // side), side * side * depth)


def split_heads(qkv_window):
    count = qkv_window.shape[0]
    parts = qkv_window.reshape(count, 3, HEADS, HEAD)
    return (parts[:, 0], parts[:, 1], parts[:, 2])


def attention_probs(query, keys, region):
    scores = jnp.einsum("qhd,khd->hqk", query, keys, preferred_element_type=jnp.float32) * HEAD ** (
        -0.5
    )
    allowed = region[:, None] == region[None, :]
    scores = jnp.where(allowed[None], scores, -1e30)
    peak = jnp.max(scores, axis=-1, keepdims=True)
    weights = jnp.exp(scores - peak)
    return weights / jnp.sum(weights, axis=-1, keepdims=True)


def forward_window(operands):
    qkv_window, region = operands
    query, keys, values = split_heads(qkv_window)
    probs = attention_probs(query, keys, region).astype(jnp.bfloat16)
    mixed = jnp.einsum("hqk,khd->qhd", probs, values, preferred_element_type=jnp.float32)
    return mixed.reshape(qkv_window.shape[0], HEADS * HEAD).astype(jnp.bfloat16)


def backward_window(operands):
    qkv_window, region, grad_window = operands
    count = qkv_window.shape[0]
    query, keys, values = split_heads(qkv_window)
    probs = attention_probs(query, keys, region)
    rounded = probs.astype(jnp.bfloat16)
    grad_heads = grad_window.reshape(count, HEADS, HEAD)
    grad_probs = jnp.einsum("qhd,khd->hqk", grad_heads, values, preferred_element_type=jnp.float32)
    grad_values = jnp.einsum(
        "hqk,qhd->khd", rounded, grad_heads, preferred_element_type=jnp.float32
    )
    inner = jnp.sum(grad_probs * probs, axis=-1, keepdims=True)
    grad_scores = (probs * (grad_probs - inner) * HEAD ** (-0.5)).astype(jnp.bfloat16)
    grad_query = jnp.einsum("hqk,khd->qhd", grad_scores, keys, preferred_element_type=jnp.float32)
    grad_keys = jnp.einsum("hqk,qhd->khd", grad_scores, query, preferred_element_type=jnp.float32)
    joined = jnp.stack([grad_query, grad_keys, grad_values], axis=1)
    return joined.reshape(count, 3 * HEADS * HEAD).astype(jnp.bfloat16)


def shards(fields, region_ids, w_qkv, w_proj, grad_output):
    rows, cols, depth, width = fields.shape
    side = WIN
    half = side // 2
    count = rows * cols * depth
    factor = float(count * lax.axis_size(LON) * lax.axis_size(LAT)) ** (-0.5)
    qkv_local = w_qkv.shape[0]
    proj_local = w_proj.shape[0]
    strip_fields, strip_grads = shifted_2((fields[:, :half], grad_output[:, :half]), LON, -1)
    moved_fields = jnp.concatenate([fields[:, half:], strip_fields], axis=1)
    moved_grads = jnp.concatenate([grad_output[:, half:], strip_grads], axis=1)
    band_fields, band_grads = shifted_2((moved_fields[:half], moved_grads[:half]), LAT, -1)
    shifted = jnp.concatenate([moved_fields[half:], band_fields], axis=0)
    grad_shift = jnp.concatenate([moved_grads[half:], band_grads], axis=0)
    flat = shifted.reshape(count, width).astype(jnp.float32)
    centre = flat - jnp.mean(flat, axis=-1, keepdims=True)
    inverse = lax.rsqrt(jnp.mean(centre * centre, axis=-1, keepdims=True) + EPSILON)
    normal = centre * inverse
    normed = normal.astype(jnp.bfloat16)
    whole_qkv, whole_proj = gather_together((w_qkv, w_proj), LON_LAT, (0, 0))
    qkv = jnp.dot(normed, whole_qkv.T, preferred_element_type=jnp.float32).astype(jnp.bfloat16)
    regions = window_regions(region_ids, cols, depth, side)
    qkv_windows = to_windows(qkv.reshape(rows, cols, depth, 3 * width), side)
    attended_windows = lax.map(forward_window, (qkv_windows, regions))
    attended = from_windows(attended_windows, rows, cols, side).reshape(count, width)
    grad_flat = grad_shift.reshape(count, width)
    branch = jnp.dot(attended, whole_proj.T, preferred_element_type=jnp.float32)
    grad_attended = jnp.dot(grad_flat, whole_proj, preferred_element_type=jnp.float32)
    branch = branch.astype(jnp.bfloat16)
    grad_attended = grad_attended.astype(jnp.bfloat16)
    grad_windows = to_windows(grad_attended.reshape(rows, cols, depth, width), side)
    grad_qkv_windows = lax.map(backward_window, (qkv_windows, regions, grad_windows))
    grad_qkv = from_windows(grad_qkv_windows, rows, cols, side).reshape(count, 3 * width)
    block_rows = qkv_local + proj_local
    owners = block_rows * lax.axis_size(LON_LAT) // block_rows
    section = grad_qkv
    qkv_part = jnp.dot(section.T, normed, preferred_element_type=jnp.float32) * factor
    section = grad_flat
    proj_part = jnp.dot(section.T, attended, preferred_element_type=jnp.float32) * factor
    stacked = jnp.concatenate(
        [qkv_part.reshape(owners, qkv_local, width), proj_part.reshape(owners, proj_local, width)],
        axis=1,
    )
    combined = spread_scatter(
        stacked.reshape(block_rows * lax.axis_size(LON_LAT), width), LON_LAT, 0
    )
    grad_w_qkv = combined[:qkv_local]
    grad_w_proj = combined[qkv_local:]
    grad_normed = jnp.dot(grad_qkv, whole_qkv, preferred_element_type=jnp.float32)
    grad_pre = inverse * (
        grad_normed
        - jnp.mean(grad_normed, axis=-1, keepdims=True)
        - normal * jnp.mean(grad_normed * normal, axis=-1, keepdims=True)
    )
    grad_pre = grad_pre.astype(jnp.bfloat16).reshape(rows, cols, depth, width)
    branch_grid = branch.reshape(rows, cols, depth, width)
    edge_branch, edge_grads = shifted_2((branch_grid[:, -half:], grad_pre[:, -half:]), LON, 1)
    placed_branch = jnp.concatenate([edge_branch, branch_grid[:, :-half]], axis=1)
    placed_grads = jnp.concatenate([edge_grads, grad_pre[:, :-half]], axis=1)
    rim_branch, rim_grads = shifted_2((placed_branch[-half:], placed_grads[-half:]), LAT, 1)
    branch_back = jnp.concatenate([rim_branch, placed_branch[:-half]], axis=0)
    grad_back = jnp.concatenate([rim_grads, placed_grads[:-half]], axis=0)
    block_out = (fields.astype(jnp.float32) + branch_back.astype(jnp.float32)).astype(jnp.bfloat16)
    grad_fields = (grad_output.astype(jnp.float32) + grad_back.astype(jnp.float32)).astype(
        jnp.bfloat16
    )
    return (block_out, grad_fields, grad_w_qkv, grad_w_proj)


def solution(mesh):
    finer = Mesh(mesh.devices.reshape(2, 4, 2, 4, 2), ("lon_0", "lon_1", "lon_2", "lat_0", "lat_1"))
    return jax.shard_map(
        shards,
        mesh=finer,
        in_specs=(
            P(LAT, LON, None, None),
            P(LAT),
            P(LON_LAT, None),
            P(LON_LAT, None),
            P(LAT, LON, None, None),
        ),
        out_specs=(
            P(LAT, LON, None, None),
            P(LAT, LON, None, None),
            P(LON_LAT, None),
            P(LON_LAT, None),
        ),
        check_vma=False,
    )
```

profile of v0, /device:TPU:0, one launch (start us, length us, event | category | flops | bytes accessed | tf_op | source)
XLA Modules:
  0.0 1117.2 jit_solution(2130976235850789125)
XLA Ops:
  54.3 264.1 %all-gather.3.cloned.1.call-done = bf16[1048576]{0:T(1024)(128)(2,1)} async-done(((bf16[8192]{0:T(1024)(128)(2,1)}), bf16[1048576]{0:T(1024)(128)(2,1)}) %all-gather.3.cloned.1.call-update) | async-done | bytes 2097168 | tf_op jit(solution)/shard_map/all_gather | solution.py:32
  326.9 7.2 convolution_convert_fusion
  334.1 12.9 %reshape_reshape.22 = bf16[2,12,2,12,3,1536]{5,4,3,2,1,0:T(4,128)(2,1)} reshape(bf16[1728,1536]{1,0:T(8,128)(2,1)} %convolution_convert_fusion) | data formatting | bytes 10616832 | tf_op jit(solution)/shard_map/reshape;reshape | solution.py:76
  347.1 13.6 %copy.58 = bf16[2,2,12,12,3,1536]{5,1,0,4,3,2:T(2,128)(2,1)} copy(bf16[2,2,12,12,3,1536]{5,4,3,1,2,0:T(4,128)(2,1)} %bitcast.179) | data formatting | bytes 10616832 | tf_op jit(solution)/shard_map/transpose | solution.py:77
  360.7 12.6 %reshape.309 = bf16[4,432,1536]{2,0,1:T(4,128)(2,1)} reshape(bf16[2,2,12,12,3,1536]{5,1,0,4,3,2:T(2,128)(2,1)} %copy.58) | data formatting | bytes 10616832 | tf_op jit(solution)/shard_map/reshape | solution.py:77
  373.3 10.5 copy.59
  402.5 161.5 %while.21 = (s32[]{:T(128)}, bf16[4,432,1536]{1,2,0:T(8,128)(2,1)}, bf16[4,432,1536]{1,2,0:T(8,128)(2,1)}, s32[4,432]{1,0:T(4,128)S(1)}, bf16[4,432,512]{1,2,0:T(8,128)(2,1)}, /*index=5*/s32[]{:T(128)}) while((s32[]{:T(128)}, bf16[4,432,1536]{1,2,0:T(8,128)(2,1)}, bf16[4,432,1536]{1,2,0:T(8,128)(2,1)}, s32[4,432]{1,0:T(4,128)S(1)}, ...), condition=%wide.region_10.11_spmd, body=%wide.region_6.10_spmd.sunk | while | flops 987560256 | bytes 89054096 | solution.py:170
  414.8 12.0 %fusion.103 = bf16[432,1,8,64]{0,3,2,1:T(8,128)(2,1)S(1)} fusion(f32[8,432,432]{1,2,0:T(8,128)} %fusion.101, bf16[432,3,8,64]{0,3,2,1:T(8,128)(2,1)S(1)} %bitcast.173, f32[8,432,432]{1,2,0:T(8,128)} %get-tuple-element.196, f32[8,432]{1,0:T(8,128)S(1)} %get-tuple-element.197), kind=kOutput, calls=%fused_computation.43.clone.1 | convolution fusion | flops 201778992 | bytes 29310976 | tf_op jit(solution)/shard_map/while/body/eval_jaxpr/hqk,khd->qhd/dot_general | solution.py:133
  426.8 10.4 fusion.102
  455.2 12.0 %fusion.103 = bf16[432,1,8,64]{0,3,2,1:T(8,128)(2,1)S(1)} fusion(f32[8,432,432]{1,2,0:T(8,128)} %fusion.101, bf16[432,3,8,64]{0,3,2,1:T(8,128)(2,1)S(1)} %bitcast.173, f32[8,432,432]{1,2,0:T(8,128)} %get-tuple-element.196, f32[8,432]{1,0:T(8,128)S(1)} %get-tuple-element.197), kind=kOutput, calls=%fused_computation.43.clone.1 | convolution fusion | flops 201778992 | bytes 29310976 | tf_op jit(solution)/shard_map/while/body/eval_jaxpr/hqk,khd->qhd/dot_general | solution.py:133
  467.2 10.4 fusion.102
  495.5 12.0 %fusion.103 = bf16[432,1,8,64]{0,3,2,1:T(8,128)(2,1)S(1)} fusion(f32[8,432,432]{1,2,0:T(8,128)} %fusion.101, bf16[432,3,8,64]{0,3,2,1:T(8,128)(2,1)S(1)} %bitcast.173, f32[8,432,432]{1,2,0:T(8,128)} %get-tuple-element.196, f32[8,432]{1,0:T(8,128)S(1)} %get-tuple-element.197), kind=kOutput, calls=%fused_computation.43.clone.1 | convolution fusion | flops 201778992 | bytes 29310976 | tf_op jit(solution)/shard_map/while/body/eval_jaxpr/hqk,khd->qhd/dot_general | solution.py:133
  507.5 10.4 fusion.102
  535.9 12.0 %fusion.103 = bf16[432,1,8,64]{0,3,2,1:T(8,128)(2,1)S(1)} fusion(f32[8,432,432]{1,2,0:T(8,128)} %fusion.101, bf16[432,3,8,64]{0,3,2,1:T(8,128)(2,1)S(1)} %bitcast.173, f32[8,432,432]{1,2,0:T(8,128)} %get-tuple-element.196, f32[8,432]{1,0:T(8,128)S(1)} %get-tuple-element.197), kind=kOutput, calls=%fused_computation.43.clone.1 | convolution fusion | flops 201778992 | bytes 29310976 | tf_op jit(solution)/shard_map/while/body/eval_jaxpr/hqk,khd->qhd/dot_general | solution.py:133
  547.9 10.4 fusion.102
  564.0 10.3 copy.74
  574.3 11.5 %reshape.315 = bf16[2,2,12,12,3,1536]{5,1,0,4,3,2:T(2,128)(2,1)} reshape(bf16[4,432,1536]{2,0,1:T(4,128)(2,1)} %copy.74) | data formatting | bytes 10616832 | tf_op jit(solution)/shard_map/reshape | solution.py:83
  585.8 9.5 copy.75
  595.3 13.7 %reshape_reshape.26 = bf16[1728,1536]{1,0:T(8,128)(2,1)} reshape(bf16[2,12,2,12,3,1536]{5,4,3,2,1,0:T(4,128)(2,1)} %copy.75) | data formatting | bytes 10616832 | tf_op jit(solution)/shard_map/reshape;reshape | solution.py:171
  609.0 47.3 %while.20 = (s32[]{:T(128)}, bf16[4,432,512]{1,2,0:T(8,128)(2,1)}, bf16[4,432,1536]{1,2,0:T(8,128)(2,1)}, s32[4,432]{1,0:T(4,128)S(1)}, s32[]{:T(128)}) while((s32[]{:T(128)}, bf16[4,432,512]{1,2,0:T(8,128)(2,1)}, bf16[4,432,1536]{1,2,0:T(8,128)(2,1)}, s32[4,432]{1,0:T(4,128)S(1)}, s32[]{:T(128)}) %tuple.87), condition=%wide.region_5.6_spmd, body=%wide.region_2.5_spmd.sunk | while | flops 391572160 | bytes 18023812 | solution.py:162
  680.3 6.8 fusion.65
  687.1 30.2 %all-reduce.46.cloned.1.call-done = f32[128,4,512]{2,1,0:T(4,128)} async-done(((f32[128,4,512]{2,1,0:T(4,128)}), f32[128,4,512]{2,1,0:T(4,128)}) %all-reduce.46.cloned.1.call-update) | async-done | bytes 1048592
  722.5 55.7 %all-reduce.60.cloned.1.call-done = (f32[128,3,512]{2,1,0:T(4,128)}, f32[64,4,512]{2,1,0:T(4,128)}) async-done(((f32[128,3,512]{2,1,0:T(4,128)}, f32[64,4,512]{2,1,0:T(4,128)}), (f32[128,3,512]{2,1,0:T(4,128)}, f32[64,4,512]{2,1,0:T(4,128)})) %all-reduce.60.cloned.1.call-update) | async-done | bytes 1310736
  798.8 8.1 fusion.62
  807.5 30.2 %all-reduce.54.cloned.1.call-done = (f32[128,3,512]{2,1,0:T(4,128)}, f32[64,3,512]{2,1,0:T(4,128)}, f32[32,4,512]{2,1,0:T(4,128)}) async-done(((f32[128,3,512]{2,1,0:T(4,128)}, f32[64,3,512]{2,1,0:T(4,128)}, f32[32,4,512]{2,1,0:T(4,128)}), (f32[128,3,512]{2,1,0:T(4,128)}, f32[64,3,512]{2,1,0:T(4,128)}, f32[32,4,512]{2,1,0:T(4,128)})) %all-reduce.54.cloned.1.call-update) | async-done | bytes 1441808
  906.9 28.4 %all-reduce.48.cloned.1.call-done = (f32[8,3,512]{2,1,0:T(4,128)}, f32[4,4,512]{2,1,0:T(4,128)}) async-done(((f32[8,3,512]{2,1,0:T(4,128)}, f32[4,4,512]{2,1,0:T(4,128)}), (f32[8,3,512]{2,1,0:T(4,128)}, f32[4,4,512]{2,1,0:T(4,128)})) %all-reduce.48.cloned.1.call-update) | async-done | bytes 81936
  937.8 53.1 %all-reduce.50.cloned.1.call-done = (f32[128,3,512]{2,1,0:T(4,128)}, f32[64,3,512]{2,1,0:T(4,128)}, f32[16,3,512]{2,1,0:T(4,128)}) async-done(((f32[128,3,512]{2,1,0:T(4,128)}, f32[64,3,512]{2,1,0:T(4,128)}, f32[16,3,512]{2,1,0:T(4,128)}), (f32[128,3,512]{2,1,0:T(4,128)}, f32[64,3,512]{2,1,0:T(4,128)}, f32[16,3,512]{2,1,0:T(4,128)})) %all-reduce.50.cloned.1.call-update) | async-done | bytes 1277968
  995.0 12.2 %all-reduce.29 = (f32[4,3,512]{2,1,0:T(4,128)S(1)}, f32[2,3,512]{2,1,0:T(4,128)S(1)}) all-reduce(f32[4,3,512]{2,1,0:T(4,128)S(1)} %constant_dynamic-slice_fusion.18, f32[2,3,512]{2,1,0:T(4,128)S(1)} %constant_dynamic-slice_fusion.21), channel_id=11, replica_groups=mesh['lon_0'=2,'lon_1'=4,'lon_2'=2,'lat_0'=4,'lat_1'=2] {'lat_1'}, use_global_device_ids=true, to_apply=%region_21.22.clone | all-reduce | flops 9216 | bytes 73728
  1007.8 20.3 %all-reduce.56.cloned.1.call-done = (f32[32,3,512]{2,1,0:T(4,128)}, f32[16,3,512]{2,1,0:T(4,128)}) async-done(((f32[32,3,512]{2,1,0:T(4,128)}, f32[16,3,512]{2,1,0:T(4,128)}), (f32[32,3,512]{2,1,0:T(4,128)}, f32[16,3,512]{2,1,0:T(4,128)})) %all-reduce.56.cloned.1.call-update) | async-done | bytes 294928
  1030.7 8.2 all-reduce.32
  1039.5 18.6 %all-reduce.44.cloned.1.call-done = f32[16,3,512]{2,1,0:T(4,128)} async-done(((f32[16,3,512]{2,1,0:T(4,128)}), f32[16,3,512]{2,1,0:T(4,128)}) %all-reduce.44.cloned.1.call-update) | async-done | bytes 98320
  1060.3 42.9 %all-reduce.52.cloned.1.call-done = (f32[8,3,512]{2,1,0:T(4,128)}, f32[4,3,512]{2,1,0:T(4,128)}) async-done(((f32[8,3,512]{2,1,0:T(4,128)}, f32[4,3,512]{2,1,0:T(4,128)}), (f32[8,3,512]{2,1,0:T(4,128)}, f32[4,3,512]{2,1,0:T(4,128)})) %all-reduce.52.cloned.1.call-update) | async-done | bytes 73744
  (265 shorter events, 318.8 us)
Async XLA Ops:
  7.2 8.9 copy-start.3
  7.2 7.3 slice-start
  7.2 311.2 %all-gather.3.cloned.1.call-start = ((), (), s32[]{:S(2)}) async-start(), calls=%async_computation | async-start | bytes 2113536 | tf_op jit(solution)/shard_map/all_gather | solution.py:32
  9.5 707.8 %all-reduce.46.cloned.1.call-start = ((), (), s32[]{:S(2)}) async-start(), calls=%async_computation.2 | async-start | bytes 2097152
  10.8 9.5 collective-permute-start
  15.4 16.5 %collective-permute-start.4 = (bf16[24,6,3,512]{3,0,2,1:T(8,128)(2,1)}, bf16[24,6,3,512]{3,0,2,1:T(8,128)(2,1)}, u32[]{:S(2)}, u32[]{:S(2)}) collective-permute-start(bf16[24,6,3,512]{3,0,2,1:T(8,128)(2,1)} %copy.93), channel_id=1, source_target_pairs={{8,0},{16,8},{24,16},{32,24},{40,32},{48,40},{56,48},{64,56},{72,6... | collective-permute-start | bytes 1327112 | tf_op jit(solution)/shard_map/ppermute | solution.py:21
  16.9 10.5 copy-start.2
  21.4 9.2 copy-start.25
  21.4 17.0 %collective-permute-start.1 = (bf16[6,24,3,512]{3,1,2,0:T(8,128)(2,1)}, bf16[6,24,3,512]{3,1,2,0:T(8,128)(2,1)}, u32[]{:S(2)}, u32[]{:S(2)}) collective-permute-start(bf16[6,24,3,512]{3,1,2,0:T(8,128)(2,1)} %pad_maximum_fusion.8), channel_id=1, source_target_pairs={{1,0},{2,1},{3,2},{4,3},{5,4},{6,5},{7,6},{0,7},{9,8},{10,9},{11,1... | collective-permute-start | bytes 1327112 | tf_op jit(solution)/shard_map/ppermute | solution.py:21
  33.9 14.4 %collective-permute-start.5 = (bf16[6,24,3,512]{3,1,2,0:T(8,128)(2,1)}, bf16[6,24,3,512]{3,1,2,0:T(8,128)(2,1)}, u32[]{:S(2)}, u32[]{:S(2)}) collective-permute-start(bf16[6,24,3,512]{3,1,2,0:T(8,128)(2,1)} %pad_maximum_fusion.7), channel_id=1, source_target_pairs={{1,0},{2,1},{3,2},{4,3},{5,4},{6,5},{7,6},{0,7},{9,8},{10,9},{11,1... | collective-permute-start | bytes 1327112 | tf_op jit(solution)/shard_map/ppermute | solution.py:21
  34.2 7.3 copy-start
  373.3 10.5 slice-start.1
  373.3 11.6 %copy-start.8 = (bf16[1728,512]{1,0:T(8,128)(2,1)S(1)}, bf16[1728,512]{1,0:T(8,128)(2,1)}, u32[]{:S(2)}) copy-start(bf16[1728,512]{1,0:T(8,128)(2,1)} %reshape.313) | copy-start | bytes 5308420
  672.3 105.8 %all-reduce.60.cloned.1.call-start = ((), (), s32[]{:S(2)}) async-start(), calls=%async_computation.9 | async-start | bytes 3145728
  687.0 32.2 %copy-start.24 = (u32[128]{0:T(128)S(1)}, u32[128]{0:T(128)}, u32[]{:S(2)}) copy-start(u32[128]{0:T(128)} %constant.62) | copy-start | bytes 1540
  719.2 118.6 %all-reduce.54.cloned.1.call-start = ((), (), s32[]{:S(2)}) async-start(), calls=%async_computation.6 | async-start | bytes 3670016
  721.2 60.8 %copy-start.23 = (u32[128]{0:T(128)S(1)}, u32[128]{0:T(128)}, u32[]{:S(2)}) copy-start(u32[128]{0:T(128)} %constant.66) | copy-start | bytes 1540
  721.2 63.5 %copy-start.19 = (f32[24,24,3]{1,2,0:T(4,128)S(1)}, f32[24,24,3]{1,2,0:T(4,128)}, u32[]{:S(2)}) copy-start(f32[24,24,3]{1,2,0:T(4,128)} %copy-done.18) | copy-start | bytes 20740
  722.5 62.5 %copy-start.15 = (f32[24,24,3]{1,2,0:T(4,128)S(1)}, f32[24,24,3]{1,2,0:T(4,128)}, u32[]{:S(2)}) copy-start(f32[24,24,3]{1,2,0:T(4,128)} %copy-done.14) | copy-start | bytes 20740
  778.2 7.4 copy-start.1
  781.9 108.8 %all-reduce.58.cloned.1.call-start = ((), (), s32[]{:S(2)}) async-start(), calls=%async_computation.8 | async-start | bytes 3014656
  842.6 92.7 %all-reduce.48.cloned.1.call-start = ((), (), s32[]{:S(2)}) async-start(), calls=%async_computation.3 | async-start | bytes 196608
  852.1 10.4 collective-permute-start.6
  861.0 8.2 copy-start.22
  861.0 11.6 %copy-start.21 = (u32[128]{0:T(128)S(1)}, u32[128]{0:T(128)}, u32[]{:S(2)}) copy-start(u32[128]{0:T(128)} %constant.74) | copy-start | bytes 1540
  861.0 22.9 %collective-permute-start.2 = (bf16[24,6,3,512]{3,0,2,1:T(8,128)(2,1)}, bf16[24,6,3,512]{3,0,2,1:T(8,128)(2,1)}, u32[]{:S(2)}, u32[]{:S(2)}) collective-permute-start(bf16[24,6,3,512]{3,0,2,1:T(8,128)(2,1)} %copy.62), channel_id=1, source_target_pairs={{120,0},{0,8},{8,16},{16,24},{24,32},{32,40},{40,48},{48,56},{56,6... | collective-permute-start | bytes 1327112 | tf_op jit(solution)/shard_map/ppermute | solution.py:21
  865.9 22.6 %collective-permute-start.7 = (bf16[6,24,3,512]{3,1,2,0:T(8,128)(2,1)}, bf16[6,24,3,512]{3,1,2,0:T(8,128)(2,1)}, u32[]{:S(2)}, u32[]{:S(2)}) collective-permute-start(bf16[6,24,3,512]{3,1,2,0:T(8,128)(2,1)} %copy.80), channel_id=1, source_target_pairs={{7,0},{0,1},{1,2},{2,3},{3,4},{4,5},{5,6},{6,7},{15,8},{8,9},{9,10... | collective-permute-start | bytes 1327112 | tf_op jit(solution)/shard_map/ppermute | solution.py:21
  887.3 14.8 %collective-permute-start.3 = (bf16[6,24,3,512]{3,1,2,0:T(8,128)(2,1)}, bf16[6,24,3,512]{3,1,2,0:T(8,128)(2,1)}, u32[]{:S(2)}, u32[]{:S(2)}) collective-permute-start(bf16[6,24,3,512]{3,1,2,0:T(8,128)(2,1)} %copy.64), channel_id=1, source_target_pairs={{7,0},{0,1},{1,2},{2,3},{3,4},{4,5},{5,6},{6,7},{15,8},{8,9},{9,10... | collective-permute-start | bytes 1327112 | tf_op jit(solution)/shard_map/ppermute | solution.py:21
  893.5 97.3 %all-reduce.50.cloned.1.call-start = ((), (), s32[]{:S(2)}) async-start(), calls=%async_computation.4 | async-start | bytes 3407872
  897.1 131.1 %all-reduce.56.cloned.1.call-start = ((), (), s32[]{:S(2)}) async-start(), calls=%async_computation.7 | async-start | bytes 786432
  994.2 63.9 %all-reduce.44.cloned.1.call-start = ((), (), s32[]{:S(2)}) async-start(), calls=%async_computation.1 | async-start | bytes 262144
  1029.8 73.4 %all-reduce.52.cloned.1.call-start = ((), (), s32[]{:S(2)}) async-start(), calls=%async_computation.5 | async-start | bytes 196608
  (14 other events, 36.1 us)
Sparse Core Ops, SparseCore 0:
  10.3 308.0 all-gather.2
  672.5 44.7 all-reduce.45
  720.5 57.5 all-reduce.59
  782.0 55.7 all-reduce.53
  842.7 25.8 all-reduce.57
  893.7 41.5 all-reduce.47
  937.8 53.0 all-reduce.49
  994.3 33.8 all-reduce.55
  1030.7 27.3 all-reduce.43
  1061.1 41.9 all-reduce.51
where the time goes:
time: 1130 us; the launch traced here: 1120 us
  waiting for transfers between devices  551 us (49%)
  local copies, waits for them, and re-layouts  264 us (23%)
  matrix products  209 us (18%)
  between operations  28.1 us (2%)
  other arithmetic  25.5 us (2%)
  blocking collectives  23.7 us (2%)
  starting transfers between devices  15.9 us (1%)
    unnamed x19, waiting for transfers between devices  280 us
    all_gather x1, waiting for transfers between devices, gather_together(): lines, at, outs = (lax.all_gather(vector, axis), 0, [])  264 us
    dot_general x4, matrix products, backward_window(): jnp.einsum('hqk,khd->qhd', grad_scores, keys, preferred_element_type=jnp....  48 us
    sub x8, matrix products, attention_probs(): weights = jnp.exp(scores - peak)  43.9 us
    dot_general x4, matrix products, backward_window(): jnp.einsum('hqk,qhd->khd', grad_scores, query, preferred_element_type=jnp...  41.5 us
    unnamed x82, local copies, waits for them, and re-layouts  38.6 us
    unnamed x3, blocking collectives  23.7 us
  transfers between devices with their start and end apart: 18, of which 12 were waited for; matrix products, arithmetic and copies ran while one was open for 11% of the time, Pallas kernels for 0%

commit v1 on v0

v1 whole, which is shorter than its diff:
```python
import jax
import jax.numpy as jnp
import numpy as np
from jax import lax
from jax.experimental import pallas as pl
from jax.experimental.pallas import tpu as pltpu
from jax.sharding import PartitionSpec as P

F32 = jnp.float32
BF = jnp.bfloat16
EPSILON = 1e-05
SLOT = 112
N = 4 * SLOT
C = 512
BLK = 112
FACTOR = float(221184) ** (-0.5)
MESH = pl.DeviceIdType.MESH
AG_ORDER = (("z", "x", "y"), ("z", "y", "x"), ("z", "x", "y"), ("z", "y", "x"))
RS_ORDER = (("y", "x", "z"), ("x", "y", "z"), ("y", "x", "z"), ("x", "y", "z"))


def nt(a, b):
    return lax.dot_general(a, b, (((1,), (1,)), ((), ())), preferred_element_type=F32)


def nn(a, b):
    return lax.dot_general(a, b, (((1,), (0,)), ((), ())), preferred_element_type=F32)


def tn(a, b):
    return lax.dot_general(a, b, (((0,), (0,)), ((), ())), preferred_element_type=F32)


def cut_matrix():
    cut = np.zeros((N, 432), np.float32)
    for q in range(4):
        for r in range(6):
            for level in range(3):
                for c in range(6):
                    cut[q * SLOT + r * 18 + level * 6 + c, (r * 3 + level) * 24 + 6 * q + c] = 1
    return cut


def unpack_matrix():
    pick = np.zeros((256, 256), np.float32)
    for s in range(16):
        for r in range(12):
            pick[12 * s + r, 16 * s + r] = 1
        for r in range(4):
            pick[192 + 4 * s + r, 16 * s + 12 + r] = 1
    return pick


class Place:
    def __init__(self):
        self.lon = lax.axis_index("lon")
        self.lat = lax.axis_index("lat")
        self.zlo = self.lon // 8
        self.x = (self.lon // 2) % 4
        self.core = self.lon % 2
        self.y = self.lat // 2
        self.zhi = self.lat % 2
        self.z = self.zhi * 2 + self.zlo

    def at(self, x=None, y=None, z=None, core=None):
        x = self.x if x is None else x
        y = self.y if y is None else y
        z = self.z if z is None else z
        core = self.core if core is None else core
        return (((z % 2) * 4 + x) * 2 + core, y * 2 + z // 2)

    def along(self, dim, step):
        there = (getattr(self, dim) + step) % 4
        return there, self.at(**{dim: there})

    def beside(self, east, south):
        return ((self.lon + east + 16) % 16, (self.lat + south + 8) % 8)


def token_regions(reg_row, half):
    def row_of(tok):
        quarter = tok // SLOT
        inside = tok - quarter * SLOT
        row = (quarter // 2) * 6 + inside // 18
        return jnp.where(inside < 108, row + 12 * half, 127)

    cols = lax.broadcasted_iota(jnp.int32, (N, 128), 1)
    toks = lax.broadcasted_iota(jnp.int32, (N, 128), 0)
    hot = (row_of(toks) == cols).astype(F32)
    col = jnp.sum(hot * reg_row, axis=1, keepdims=True)
    row = nt(jnp.broadcast_to(reg_row, (8, 128)).astype(BF), hot.astype(BF))[0:1]
    return col, row


def normalised(x):
    xf = x.astype(F32)
    centre = xf - jnp.mean(xf, axis=-1, keepdims=True)
    inverse = lax.rsqrt(jnp.mean(centre * centre, axis=-1, keepdims=True) + EPSILON)
    return centre * inverse, inverse


def window(w, half, which, xg, reg_s, wq, wp, ow, normed_s, att_s, gqkv_s, qkv_s, ga_s, bias_s, r_s, t_s):
    normal, inverse = normalised(xg[0, w].reshape(N, C))
    normed = normal.astype(BF)
    normed_s[w] = normed
    col, row = token_regions(reg_s[which, 0:1, :], half)
    bias_s[...] = jnp.where(col == row, 0.0, -1e30)
    qkv_s[:, :512] = nt(normed, wq[0:512, :]).astype(BF) * jnp.asarray(0.125, BF)
    qkv_s[:, 512:1024] = nt(normed, wq[512:1024, :]).astype(BF)
    qkv_s[:, 1024:] = nt(normed, wq[1024:, :]).astype(BF)
    ga_s[...] = nn(xg[1, w].reshape(N, C), wp[...]).astype(BF)
    low = lax.broadcasted_iota(jnp.int32, (N, 128), 1) < 64

    def pair(hp, _):
        o = pl.multiple_of(hp * 128, 128)
        q2 = qkv_s[:, pl.ds(o, 128)]
        k2 = qkv_s[:, pl.ds(512 + o, 128)]
        v2 = qkv_s[:, pl.ds(1024 + o, 128)]
        g2 = ga_s[:, pl.ds(o, 128)]
        outs = []
        for h in range(2):
            keep = low if h == 0 else jnp.logical_not(low)
            qa = jnp.where(keep, q2, jnp.zeros_like(q2))
            gaa = jnp.where(keep, g2, jnp.zeros_like(g2))
            for b in range(0, N, BLK):
                s = nt(qa[b : b + BLK], k2) + bias_s[b : b + BLK, :]
                m = jnp.max(s, axis=-1, keepdims=True)
                e = jnp.exp(s - m)
                p = e * (1.0 / jnp.sum(e, axis=-1, keepdims=True))
                r_s[h, b : b + BLK, :] = p.astype(BF)
                dp = nt(gaa[b : b + BLK], v2)
                inner = jnp.sum(dp * p, axis=-1, keepdims=True)
                t_s[h, b : b + BLK, :] = (p * (dp - inner)).astype(BF)
            r = r_s[h]
            t = t_s[h]
            outs.append((nn(r, v2), nn(t, k2), tn(t, q2), tn(r, g2)))
        att, dq, dk, dv = [jnp.where(low, a, b) for a, b in zip(*outs)]
        att_s[w, :, pl.ds(o, 128)] = att.astype(BF)
        gqkv_s[w, :, pl.ds(o, 128)] = (dq * 0.125).astype(BF)
        gqkv_s[w, :, pl.ds(512 + o, 128)] = dk.astype(BF)
        gqkv_s[w, :, pl.ds(1024 + o, 128)] = dv.astype(BF)
        return 0

    lax.fori_loop(0, 4, pair, 0)
    ow[0, w] = nt(att_s[w], wp[...]).astype(BF).reshape(4, SLOT, C)
    grad = nn(gqkv_s[w], wq[...])
    normal, inverse = normalised(xg[0, w].reshape(N, C))
    grad = inverse * (
        grad
        - jnp.mean(grad, axis=-1, keepdims=True)
        - normal * jnp.mean(grad * normal, axis=-1, keepdims=True)
    )
    ow[1, w] = grad.astype(BF).reshape(4, SLOT, C)


def kernel(
    f_ref, g_ref, reg_ref, wq_ref, wp_ref, cut_ref, paste_ref, pick_ref, pack_ref,
    fo_ref, go_ref, qo_ref, po_ref,
    own_s, wg, wq, wp, stage, xg, reg_s, ow, rq,
    normed_s, att_s, gqkv_s, qkv_s, ga_s, bias_s, r_s, t_s,
    gw_s, pk, rc, h0, rb0, h1, rb1, h2, rb2,
    ag_a, ag_b, in_a, in_b, out_a, out_b, rc_a, rc_b, rs_a, rs_b,
):
    me = Place()
    sibling = me.at(core=1 - me.core)

    def copy(src, dst, a, b, device):
        return pltpu.make_async_remote_copy(
            src_ref=src, dst_ref=dst, send_sem=a, recv_sem=b, device_id=device, device_id_type=MESH
        )

    barrier = pltpu.get_barrier_semaphore()
    greeted = [me.along(d, s)[1] for d in ("x", "y", "z") for s in (1, 2, 3)] + [sibling]
    greeted += [me.beside(*o) for o in ((-1, 0), (1, 0), (0, -1), (0, 1), (1, 1), (-1, -1))]
    for device in greeted:
        pl.semaphore_signal(barrier, inc=1, device_id=device, device_id_type=MESH)

    own_s[0:12, :] = wq_ref[...].astype(F32)
    own_s[12:16, :] = wp_ref[...].astype(F32)
    for k in range(4):
        wg[k, me.zlo, me.x, me.core, me.y, me.zhi] = own_s[:, 128 * k : 128 * k + 128].astype(BF)
    reg_s[0] = reg_ref[...]
    pl.semaphore_wait(barrier, len(greeted))

    every = slice(None)

    def held(k, done):
        return wg.at[
            k,
            every if "z" in done else me.zlo,
            every if "x" in done else me.x,
            every if "core" in done else me.core,
            every if "y" in done else me.y,
            every if "z" in done else me.zhi,
        ]

    gathers = []

    def gather_step(stage_index):
        for k in range(4):
            if stage_index > 0:
                for c in gathers[-4 if k == 0 else -4]:
                    c.wait_recv()
            if stage_index < 3:
                order = AG_ORDER[k]
                part = held(k, order[:stage_index])
                started = []
                for step in (1, 2, 3):
                    sem = k * 9 + stage_index * 3 + step - 1
                    started.append(copy(part, part, ag_a.at[sem], ag_b.at[sem], me.along(order[stage_index], step)[1]))
            else:
                part = held(k, ("x", "y", "z"))
                started = [copy(part, part, ag_a.at[36 + k], ag_b.at[36 + k], sibling)]
            for c in started:
                c.start()
            gathers.append(started)

    halos = {}

    def cut(qi, moves):
        for a, ref in ((0, f_ref), (1, g_ref)):
            rows = nn(cut_ref[...], ref[432 * qi : 432 * qi + 432, :]).astype(BF)
            for qj in range(4):
                quarter = rows[SLOT * qj : SLOT * qj + SLOT]
                where = moves[qj]
                if where[0] == "own":
                    xg[a, where[1], where[2]] = quarter
                else:
                    stage[a, where[1]] = quarter

    def send_in(name, slots, w, first, count, device, sem):
        c = copy(
            stage.at[:, pl.ds(slots, count)], xg.at[:, w, pl.ds(first, count)], in_a.at[sem], in_b.at[sem], device
        )
        c.start()
        halos.setdefault(name, []).append(c)

    gather_step(0)
    cut(0, (("own", 3, 3), ("out", 0), ("out", 1), ("out", 2)))
    send_in("s", 0, 2, 2, 2, me.beside(0, -1), 0)
    send_in("c", 2, 3, 2, 1, me.beside(1, 0), 1)
    c = copy(reg_s.at[0], reg_s.at[1], in_a.at[6], in_b.at[6], me.beside(0, 1))
    c.start()
    halos["c"].append(c)
    gather_step(1)
    cut(3, (("out", 3), ("own", 2, 0), ("own", 2, 1), ("out", 4)))
    send_in("c", 3, 3, 1, 1, me.beside(0, 1), 2)
    send_in("c", 4, 3, 0, 1, me.beside(1, 1), 3)
    gather_step(2)
    cut(1, (("out", 5), ("own", 0, 0), ("own", 0, 1), ("own", 1, 0)))
    send_in("e", 5, 1, 1, 1, me.beside(-1, 0), 4)
    cut(2, (("out", 6), ("own", 0, 2), ("own", 0, 3), ("own", 1, 2)))
    send_in("e", 6, 1, 3, 1, me.beside(-1, 0), 5)
    gather_step(3)
    for started in gathers[-4:]:
        started[0].wait_recv()

    def unpack(j, _):
        for half in range(2):
            parts = [wg[2 * half + k, j // 4, j % 4].reshape(256, 128) for k in range(2)]
            got = nn(pick_ref[...], jnp.concatenate(parts, axis=1)).astype(BF)
            wq[pl.ds(pl.multiple_of(192 * j, 64), 192), 256 * half : 256 * half + 256] = got[:192]
            wp[pl.ds(pl.multiple_of(64 * j, 64), 64), 256 * half : 256 * half + 256] = got[192:]
        return 0

    lax.fori_loop(0, 8, unpack, 0)

    def send_out(w, first, qi, qj, count, device, sem):
        return copy(
            ow.at[:, w, pl.ds(first, count)], rq.at[:, qi, pl.ds(qj, count)], out_a.at[sem], out_b.at[sem], device
        )

    returns = [
        send_out(2, 2, 0, 1, 2, me.beside(0, 1), 0),
        send_out(3, 2, 0, 3, 1, me.beside(-1, 0), 1),
        send_out(3, 1, 3, 0, 1, me.beside(0, -1), 2),
        send_out(3, 0, 3, 3, 1, me.beside(-1, -1), 3),
        send_out(1, 1, 1, 0, 1, me.beside(1, 0), 4),
        send_out(1, 3, 2, 0, 1, me.beside(1, 0), 5),
    ]
    leaves = {0: (4, 5), 1: (0,), 2: (1, 2, 3)}

    def turn(i, _):
        w = (i + 1) % 4
        for step, name in ((0, "e"), (1, "s"), (2, "c")):

            @pl.when(i == step)
            def _():
                for c in halos[name]:
                    c.wait_recv()

        half = jnp.where(jnp.logical_or(i == 1, i == 2), 1, 0)
        which = jnp.where(i == 2, 1, 0)
        window(w, half, which, xg, reg_s, wq, wp, ow, normed_s, att_s, gqkv_s, qkv_s, ga_s, bias_s, r_s, t_s)
        for step in range(3):

            @pl.when(i == step)
            def _():
                for number in leaves[step]:
                    returns[number].start()

        return 0

    lax.fori_loop(0, 4, turn, 0)

    normed = normed_s[...].reshape(4 * N, C)

    def weight_chunk(i, _):
        o = pl.multiple_of(i * 256, 256)
        left = gqkv_s[:, :, pl.ds(o, 256)].reshape(4 * N, 256)
        gw_s[pl.ds(o, 256), :] = (tn(left, normed) * FACTOR).astype(BF)
        return 0

    lax.fori_loop(0, 6, weight_chunk, 0)
    gw_s[1536:2048, :] = (tn(xg[1].reshape(4 * N, C), att_s[...].reshape(4 * N, C)) * FACTOR).astype(BF)

    def across(j):
        return copy(
            pk.at[:, j // 4, j % 4, 1 - me.core], rc.at[:, j // 4, j % 4], rc_a.at[j], rc_b.at[j], sibling
        )

    def pack(j, _):
        rows = jnp.concatenate(
            [
                gw_s[pl.ds(pl.multiple_of(192 * j, 64), 192), :],
                gw_s[pl.ds(pl.multiple_of(1536 + 64 * j, 64), 64), :],
            ],
            axis=0,
        )
        got = nn(pack_ref[...], rows).astype(BF)
        for k in range(4):
            pk[k, j // 4, j % 4] = got[:, 128 * k : 128 * k + 128].reshape(2, 4, 2, 16, 128)
        across(j).start()
        return 0

    lax.fori_loop(0, 8, pack, 0)

    def merge(j, _):
        across(j).wait_recv()
        mine = pk[:, j // 4, j % 4, me.core].astype(F32)
        h0[:, j // 4, j % 4] = (mine + rc[:, j // 4, j % 4].astype(F32)).astype(BF)
        return 0

    lax.fori_loop(0, 8, merge, 0)

    reduces = []

    def reduce_step(stage_index):
        for k in range(4):
            order = RS_ORDER[k]
            started = []
            for step in (1, 2, 3):
                there, device = me.along(order[stage_index], step)
                if stage_index == 0:
                    src = h0.at[k, :, :, there] if order[0] == "y" else h0.at[k, :, there]
                    dst = rb0.at[k, step - 1]
                elif stage_index == 1:
                    src, dst = h1.at[k, :, there], rb1.at[k, step - 1]
                else:
                    src, dst = h2.at[k, there % 2, there // 2], rb2.at[k, step - 1]
                sem = k * 9 + stage_index * 3 + step - 1
                c = copy(src, dst, rs_a.at[sem], rs_b.at[sem], device)
                c.start()
                started.append(c)
            reduces.append(started)

    def reduce_take(stage_index):
        for k in range(4):
            order = RS_ORDER[k]
            for c in reduces[4 * stage_index + k]:
                c.wait_recv()
            got = (rb0, rb1, rb2)[stage_index]
            if stage_index == 0:
                mine = h0[k, :, :, me.y] if order[0] == "y" else h0[k, :, me.x]
            elif stage_index == 1:
                mine = h1[k, :, getattr(me, order[1])]
            else:
                mine = h2[k, me.zlo, me.zhi]
            total = mine.astype(F32)
            for step in range(3):
                total = total + got[k, step].astype(F32)
            if stage_index == 0:
                h1[k] = total.astype(BF)
            elif stage_index == 1:
                h2[k] = total.astype(BF)
            else:
                own_s[:, 128 * k : 128 * k + 128] = total

    mine = {
        (1, 1): (0, 0), (1, 2): (0, 1), (2, 1): (0, 2), (2, 2): (0, 3), (1, 3): (1, 0),
        (2, 3): (1, 2), (3, 1): (2, 0), (3, 2): (2, 1), (0, 0): (3, 3),
    }

    def paste(qi):
        for a, ref, out in ((0, f_ref, fo_ref), (1, g_ref, go_ref)):
            quarters = []
            for qj in range(4):
                if (qi, qj) in mine:
                    quarters.append(ow[(a,) + mine[(qi, qj)]])
                else:
                    quarters.append(rq[a, qi, qj])
            back = nn(paste_ref[...], jnp.concatenate(quarters, axis=0))
            rows = slice(432 * qi, 432 * qi + 432)
            out[rows, :] = (ref[rows, :].astype(F32) + back).astype(BF)

    reduce_step(0)
    for c in returns:
        c.wait_recv()
    paste(1)
    paste(2)
    reduce_take(0)
    reduce_step(1)
    paste(0)
    reduce_take(1)
    reduce_step(2)
    paste(3)
    reduce_take(2)
    qo_ref[...] = own_s[0:12, :]
    po_ref[...] = own_s[12:16, :]

    for started in gathers + reduces + [returns] + list(halos.values()):
        for c in started:
            c.wait_send()
    for j in range(8):
        across(j).wait_send()


def shards(fields, region_ids, w_qkv, w_proj, grad_output):
    tokens = 24 * 24 * 3
    flat = fields.transpose(0, 2, 1, 3).reshape(tokens, C)
    grad = grad_output.transpose(0, 2, 1, 3).reshape(tokens, C)
    regions = jnp.broadcast_to(jnp.pad((region_ids + 1).astype(F32), (0, 104))[None], (8, 128))
    cut = cut_matrix()
    pick = unpack_matrix()
    vm = pl.BlockSpec(memory_space=pltpu.VMEM)
    shape = jax.ShapeDtypeStruct
    dma = pltpu.SemaphoreType.DMA
    fo, go, qo, po = pl.pallas_call(
        kernel,
        out_shape=(shape((tokens, C), BF), shape((tokens, C), BF), shape((12, C), F32), shape((4, C), F32)),
        in_specs=[vm] * 9,
        out_specs=[vm] * 4,
        scratch_shapes=[
            pltpu.VMEM((16, C), F32),
            pltpu.VMEM((4, 2, 4, 2, 4, 2, 16, 128), BF),
            pltpu.VMEM((1536, C), BF),
            pltpu.VMEM((C, C), BF),
            pltpu.VMEM((2, 7, SLOT, C), BF),
            pltpu.VMEM((2, 4, 4, SLOT, C), BF),
            pltpu.VMEM((2, 8, 128), F32),
            pltpu.VMEM((2, 4, 4, SLOT, C), BF),
            pltpu.VMEM((2, 4, 4, SLOT, C), BF),
            pltpu.VMEM((4, N, C), BF),
            pltpu.VMEM((4, N, C), BF),
            pltpu.VMEM((4, N, 3 * C), BF),
            pltpu.VMEM((N, 3 * C), BF),
            pltpu.VMEM((N, C), BF),
            pltpu.VMEM((N, N), F32),
            pltpu.VMEM((2, N, N), BF),
            pltpu.VMEM((2, N, N), BF),
            pltpu.VMEM((2048, C), BF),
            pltpu.VMEM((4, 2, 4, 2, 4, 2, 16, 128), BF),
            pltpu.VMEM((4, 2, 4, 4, 2, 16, 128), BF),
            pltpu.VMEM((4, 2, 4, 4, 2, 16, 128), BF),
            pltpu.VMEM((4, 3, 2, 4, 2, 16, 128), BF),
            pltpu.VMEM((4, 2, 4, 2, 16, 128), BF),
            pltpu.VMEM((4, 3, 2, 2, 16, 128), BF),
            pltpu.VMEM((4, 2, 2, 16, 128), BF),
            pltpu.VMEM((4, 3, 16, 128), BF),
            dma((40,)), dma((40,)), dma((7,)), dma((7,)), dma((6,)), dma((6,)),
            dma((8,)), dma((8,)), dma((36,)), dma((36,)),
        ],
        compiler_params=pltpu.CompilerParams(
            collective_id=0, has_side_effects=True, vmem_limit_bytes=60 * 1024 * 1024
        ),
        name="block",
    )(
        flat, grad, regions, w_qkv, w_proj,
        jnp.asarray(cut, BF), jnp.asarray(cut.T, BF), jnp.asarray(pick, BF), jnp.asarray(pick.T, BF),
    )
    block_out = fo.reshape(24, 3, 24, C).transpose(0, 2, 1, 3)
    grad_fields = go.reshape(24, 3, 24, C).transpose(0, 2, 1, 3)
    return block_out, grad_fields, qo, po


def solution(mesh):
    return jax.shard_map(
        shards,
        mesh=mesh,
        in_specs=(
            P("lat", "lon", None, None), P("lat"), P(("lon", "lat"), None), P(("lon", "lat"), None),
            P("lat", "lon", None, None),
        ),
        out_specs=(
            P("lat", "lon", None, None), P("lat", "lon", None, None),
            P(("lon", "lat"), None), P(("lon", "lat"), None),
        ),
        check_vma=False,
    )
```

time: 1130 us -> 132 us (0.12); the launches traced: 1120 us -> 132 us
  waiting for transfers between devices: 551 us -> 0 us
  local copies, waits for them, and re-layouts: 264 us -> 5.97 us
  matrix products: 209 us -> 0 us
  Pallas kernels: 0 us -> 124 us
  between operations: 28.1 us -> 0.65 us
  other arithmetic: 25.5 us -> 0.66 us
  blocking collectives: 23.7 us -> 0 us
  starting transfers between devices: 15.9 us -> 0 us
    unnamed x19 -> x0, waiting for transfers between devices: 280 us -> none
    all_gather x1 -> x0, waiting for transfers between devices: 264 us -> none  [gather_together(): lines, at, outs = (lax.all_gather(vector, axis), 0, [])]
    dot_general x26 -> x0, matrix products: 165 us -> none  [the longest x4 48 us: backward_window(): jnp.einsum('hqk,khd->qhd', grad_scores, keys, preferred_element_type=jnp....]
    pallas_call x0 -> x1, Pallas kernels: none -> 124 us  [shards(): pl.pallas_call(kernel, out_shape=(shape((tokens, C), BF), shape((tokens,...]
    reshape x10 -> x0, local copies, waits for them, and re-layouts: 44.5 us -> none  [the longest x2 16.9 us: to_windows(): blocks.transpose(0, 2, 1, 3, 4, 5).reshape(-1, side * side * depth, width)]
    sub x8 -> x0, matrix products: 43.9 us -> none  [attention_probs(): weights = jnp.exp(scores - peak)]
    another operation x7 -> x0, local copies, waits for them, and re-layouts: 38.8 us -> none  [the longest x2 17 us: to_windows(): blocks = grid.reshape(rows // side, side, cols // side, side, depth, width)]
    transpose x8 -> x0, local copies, waits for them, and re-layouts: 37.3 us -> none  [the longest x2 17.6 us: to_windows(): blocks.transpose(0, 2, 1, 3, 4, 5).reshape(-1, side * side * depth, width)]
  transfers between devices with their start and end apart: 18 -> 0, of which waited for: 12 -> 0; matrix products, arithmetic and copies ran while one was open for 11% -> 0% of each run, Pallas kernels for 0% -> 0%
where the time goes in v1:
time: 132 us
  Pallas kernels  124 us (94%)
  local copies, waits for them, and re-layouts  5.97 us (5%)
    pallas_call x1, Pallas kernels, shards(): pl.pallas_call(kernel, out_shape=(shape((tokens, C), BF), shape((tokens,...  124 us
    unnamed x10, local copies, waits for them, and re-layouts  5.37 us

profile of v1, /device:TPU:0, one launch (start us, length us, event | category | flops | bytes accessed | tf_op | source)
XLA Modules:
  0.0 131.6 jit_solution(248167507076455193)
XLA Ops:
  0.6 0.7 add_convert_fusion
  1.3 0.6 broadcast_in_dim.2.reg_ref
  1.9 124.3 %block.1 = (bf16[1728,512]{1,0:T(8,128)(2,1)}, bf16[1728,512]{1,0:T(8,128)(2,1)}, f32[12,512]{1,0:T(8,128)}, f32[4,512]{1,0:T(4,128)}) custom-call(bf16[1728,512]{1,0:T(8,128)(2,1)} %bitcast.12, bf16[1728,512]{1,0:T(8,128)(2,1)} %bitcast.13, f32[8,128]{1,0:T(8,128)} %broadcast_in_dim.2.reg_ref, bf16[12,512]{1,0:T(8,128)(2,1)} %wq_ref.1, ...), custom_call_target="tpu_custom_call" | custom-call | tf_op jit(solution)/shard_map/block/pallas_call | solution.py:438
  126.2 0.0 copy-start
  126.2 2.9 %copy.17 = bf16[24,24,3,512]{3,1,2,0:T(8,128)(2,1)} copy(bf16[24,24,3,512]{3,1,2,0:T(8,128)(2,1)} %bitcast.15) | data formatting | bytes 3538944
  129.1 0.0 copy-done
  129.1 0.0 copy-start.1
  129.2 0.0 copy-start.2
  129.2 1.2 copy.18
  130.4 0.0 copy-done.1
  130.4 0.6 copy.19
  131.0 0.0 copy-done.2
  131.0 0.6 copy.20
  (1 shorter events, 0.0 us)
Async XLA Ops:
  126.2 2.9 %copy-start = (bf16[1728,512]{1,0:T(8,128)(2,1)S(1)}, bf16[1728,512]{1,0:T(8,128)(2,1)}, u32[]{:S(2)}) copy-start(bf16[1728,512]{1,0:T(8,128)(2,1)} %get-tuple-element.9) | copy-start | bytes 5308420
  129.1 1.2 copy-start.1
  129.2 1.8 %copy-start.2 = (f32[4,512]{1,0:T(4,128)S(1)}, f32[4,512]{1,0:T(4,128)}, u32[]{:S(2)}) copy-start(f32[4,512]{1,0:T(4,128)} %get-tuple-element.19) | copy-start | bytes 24580

commit v2 on v1

--- a/solution.py
+++ b/solution.py
@@ -154,8 +154,9 @@
 
 
 def kernel(
-    f_ref, g_ref, reg_ref, wq_ref, wp_ref, cut_ref, paste_ref, pick_ref, pack_ref,
+    f_hbm, g_hbm, reg_ref, wq_ref, wp_ref, cut_hbm, paste_hbm, pick_hbm, pack_hbm,
     fo_ref, go_ref, qo_ref, po_ref,
+    f_ref, g_ref, cut_ref, paste_ref, pick_ref, pack_ref, load_sem,
     own_s, wg, wq, wp, stage, xg, reg_s, ow, rq,
     normed_s, att_s, gqkv_s, qkv_s, ga_s, bias_s, r_s, t_s,
     gw_s, pk, rc, h0, rb0, h1, rb1, h2, rb2,
@@ -175,6 +176,18 @@
     for device in greeted:
         pl.semaphore_signal(barrier, inc=1, device_id=device, device_id_type=MESH)
 
+    loads = [
+        pltpu.make_async_copy(src, dst, load_sem.at[n])
+        for n, (src, dst) in enumerate(
+            (
+                (f_hbm, f_ref), (g_hbm, g_ref), (cut_hbm, cut_ref),
+                (pick_hbm, pick_ref), (paste_hbm, paste_ref), (pack_hbm, pack_ref),
+            )
+        )
+    ]
+    for c in loads:
+        c.start()
+
     own_s[0:12, :] = wq_ref[...].astype(F32)
     own_s[12:16, :] = wp_ref[...].astype(F32)
     for k in range(4):
@@ -184,36 +197,50 @@
 
     every = slice(None)
 
-    def held(k, done):
+    def held(k, done, **fixed):
+        z = fixed.get("z", me.z)
         return wg.at[
             k,
-            every if "z" in done else me.zlo,
-            every if "x" in done else me.x,
-            every if "core" in done else me.core,
-            every if "y" in done else me.y,
-            every if "z" in done else me.zhi,
+            every if "z" in done else z % 2,
+            every if "x" in done else fixed.get("x", me.x),
+            me.core,
+            every if "y" in done else fixed.get("y", me.y),
+            every if "z" in done else z // 2,
         ]
 
     gathers = []
+    forwards = []
+
+    def forward(k, number, part):
+        c = copy(part, part, ag_a.at[36 + 4 * k + number], ag_b.at[36 + 4 * k + number], sibling)
+        c.start()
+        forwards.append(c)
 
     def gather_step(stage_index):
         for k in range(4):
             if stage_index > 0:
-                for c in gathers[-4 if k == 0 else -4]:
+                for c in gathers[-4]:
                     c.wait_recv()
-            if stage_index < 3:
-                order = AG_ORDER[k]
-                part = held(k, order[:stage_index])
-                started = []
-                for step in (1, 2, 3):
-                    sem = k * 9 + stage_index * 3 + step - 1
-                    started.append(copy(part, part, ag_a.at[sem], ag_b.at[sem], me.along(order[stage_index], step)[1]))
-            else:
-                part = held(k, ("x", "y", "z"))
-                started = [copy(part, part, ag_a.at[36 + k], ag_b.at[36 + k], sibling)]
-            for c in started:
+            order = AG_ORDER[k]
+            part = held(k, order[:stage_index])
+            started = []
+            for step in (1, 3, 2):
+                sem = k * 9 + stage_index * 3 + step - 1
+                c = copy(part, part, ag_a.at[sem], ag_b.at[sem], me.along(order[stage_index], step)[1])
                 c.start()
+                started.append(c)
             gathers.append(started)
+            if stage_index == 2:
+                forward(k, 0, part)
+
+    def gather_end():
+        for n, step in enumerate((1, 3, 2)):
+            for k in range(4):
+                gathers[k - 4][n].wait_recv()
+                dim = AG_ORDER[k][2]
+                forward(k, step, held(k, AG_ORDER[k][:2], **{dim: me.along(dim, 4 - step)[0]}))
+        for c in forwards:
+            c.wait_recv()
 
     halos = {}
 
@@ -236,24 +263,26 @@
         halos.setdefault(name, []).append(c)
 
     gather_step(0)
+    for c in loads[:3]:
+        c.wait()
+    cut(1, (("out", 5), ("own", 0, 0), ("own", 0, 1), ("own", 1, 0)))
+    gather_step(1)
+    cut(2, (("out", 6), ("own", 0, 2), ("own", 0, 3), ("own", 1, 2)))
+    gather_step(2)
     cut(0, (("own", 3, 3), ("out", 0), ("out", 1), ("out", 2)))
+    cut(3, (("out", 3), ("own", 2, 0), ("own", 2, 1), ("out", 4)))
+    gather_end()
+    send_in("e", 5, 1, 1, 1, me.beside(-1, 0), 4)
+    send_in("e", 6, 1, 3, 1, me.beside(-1, 0), 5)
     send_in("s", 0, 2, 2, 2, me.beside(0, -1), 0)
     send_in("c", 2, 3, 2, 1, me.beside(1, 0), 1)
     c = copy(reg_s.at[0], reg_s.at[1], in_a.at[6], in_b.at[6], me.beside(0, 1))
     c.start()
     halos["c"].append(c)
-    gather_step(1)
-    cut(3, (("out", 3), ("own", 2, 0), ("own", 2, 1), ("out", 4)))
     send_in("c", 3, 3, 1, 1, me.beside(0, 1), 2)
     send_in("c", 4, 3, 0, 1, me.beside(1, 1), 3)
-    gather_step(2)
-    cut(1, (("out", 5), ("own", 0, 0), ("own", 0, 1), ("own", 1, 0)))
-    send_in("e", 5, 1, 1, 1, me.beside(-1, 0), 4)
-    cut(2, (("out", 6), ("own", 0, 2), ("own", 0, 3), ("own", 1, 2)))
-    send_in("e", 6, 1, 3, 1, me.beside(-1, 0), 5)
-    gather_step(3)
-    for started in gathers[-4:]:
-        started[0].wait_recv()
+    for c in loads[3:]:
+        c.wait()
 
     def unpack(j, _):
         for half in range(2):
@@ -278,21 +307,18 @@
         send_out(1, 1, 1, 0, 1, me.beside(1, 0), 4),
         send_out(1, 3, 2, 0, 1, me.beside(1, 0), 5),
     ]
-    leaves = {0: (4, 5), 1: (0,), 2: (1, 2, 3)}
+    leaves = {1: (4, 5), 2: (0,), 3: (1, 2, 3)}
 
     def turn(i, _):
-        w = (i + 1) % 4
-        for step, name in ((0, "e"), (1, "s"), (2, "c")):
+        for step, name in ((1, "e"), (2, "s"), (3, "c")):
 
             @pl.when(i == step)
             def _():
                 for c in halos[name]:
                     c.wait_recv()
 
-        half = jnp.where(jnp.logical_or(i == 1, i == 2), 1, 0)
-        which = jnp.where(i == 2, 1, 0)
-        window(w, half, which, xg, reg_s, wq, wp, ow, normed_s, att_s, gqkv_s, qkv_s, ga_s, bias_s, r_s, t_s)
-        for step in range(3):
+        window(i, i // 2, i // 3, xg, reg_s, wq, wp, ow, normed_s, att_s, gqkv_s, qkv_s, ga_s, bias_s, r_s, t_s)
+        for step in (1, 2, 3):
 
             @pl.when(i == step)
             def _():
@@ -392,7 +418,7 @@
     }
 
     def paste(qi):
-        for a, ref, out in ((0, f_ref, fo_ref), (1, g_ref, go_ref)):
+        for a, out in ((0, fo_ref), (1, go_ref)):
             quarters = []
             for qj in range(4):
                 if (qi, qj) in mine:
@@ -400,8 +426,7 @@
                 else:
                     quarters.append(rq[a, qi, qj])
             back = nn(paste_ref[...], jnp.concatenate(quarters, axis=0))
-            rows = slice(432 * qi, 432 * qi + 432)
-            out[rows, :] = (ref[rows, :].astype(F32) + back).astype(BF)
+            out[432 * qi : 432 * qi + 432, :] = back.astype(BF)
 
     reduce_step(0)
     for c in returns:
@@ -418,7 +443,7 @@
     qo_ref[...] = own_s[0:12, :]
     po_ref[...] = own_s[12:16, :]
 
-    for started in gathers + reduces + [returns] + list(halos.values()):
+    for started in gathers + reduces + [returns, forwards] + list(halos.values()):
         for c in started:
             c.wait_send()
     for j in range(8):
@@ -433,14 +458,22 @@
     cut = cut_matrix()
     pick = unpack_matrix()
     vm = pl.BlockSpec(memory_space=pltpu.VMEM)
+    hbm = pl.BlockSpec(memory_space=pl.ANY)
     shape = jax.ShapeDtypeStruct
     dma = pltpu.SemaphoreType.DMA
     fo, go, qo, po = pl.pallas_call(
         kernel,
         out_shape=(shape((tokens, C), BF), shape((tokens, C), BF), shape((12, C), F32), shape((4, C), F32)),
-        in_specs=[vm] * 9,
+        in_specs=[hbm] * 2 + [vm] * 3 + [hbm] * 4,
         out_specs=[vm] * 4,
         scratch_shapes=[
+            pltpu.VMEM((tokens, C), BF),
+            pltpu.VMEM((tokens, C), BF),
+            pltpu.VMEM((N, 432), BF),
+            pltpu.VMEM((432, N), BF),
+            pltpu.VMEM((256, 256), BF),
+            pltpu.VMEM((256, 256), BF),
+            dma((6,)),
             pltpu.VMEM((16, C), F32),
             pltpu.VMEM((4, 2, 4, 2, 4, 2, 16, 128), BF),
             pltpu.VMEM((1536, C), BF),
@@ -467,19 +500,21 @@
             pltpu.VMEM((4, 3, 2, 2, 16, 128), BF),
             pltpu.VMEM((4, 2, 2, 16, 128), BF),
             pltpu.VMEM((4, 3, 16, 128), BF),
-            dma((40,)), dma((40,)), dma((7,)), dma((7,)), dma((6,)), dma((6,)),
+            dma((52,)), dma((52,)), dma((7,)), dma((7,)), dma((6,)), dma((6,)),
             dma((8,)), dma((8,)), dma((36,)), dma((36,)),
         ],
         compiler_params=pltpu.CompilerParams(
-            collective_id=0, has_side_effects=True, vmem_limit_bytes=60 * 1024 * 1024
+            collective_id=0, has_side_effects=True, vmem_limit_bytes=48 * 1024 * 1024
         ),
         name="block",
     )(
         flat, grad, regions, w_qkv, w_proj,
         jnp.asarray(cut, BF), jnp.asarray(cut.T, BF), jnp.asarray(pick, BF), jnp.asarray(pick.T, BF),
     )
-    block_out = fo.reshape(24, 3, 24, C).transpose(0, 2, 1, 3)
-    grad_fields = go.reshape(24, 3, 24, C).transpose(0, 2, 1, 3)
+    block_out = (flat.astype(F32) + fo.astype(F32)).astype(BF)
+    grad_fields = (grad.astype(F32) + go.astype(F32)).astype(BF)
+    block_out = block_out.reshape(24, 3, 24, C).transpose(0, 2, 1, 3)
+    grad_fields = grad_fields.reshape(24, 3, 24, C).transpose(0, 2, 1, 3)
     return block_out, grad_fields, qo, po
 
 

time: 132 us -> 114 us (0.86)
  Pallas kernels: 124 us -> 102 us
  other arithmetic: 0.66 us -> 3.68 us
    pallas_call x1, Pallas kernels: 124 us -> 102 us  [shards(): pl.pallas_call(kernel, out_shape=(shape((tokens, C), BF), shape((tokens,...]
    convert_element_type x0 -> x1, other arithmetic: none -> 3.02 us  [shards(): grad_fields = (grad.astype(F32) + go.astype(F32)).astype(BF)]
    unnamed x10 -> x18, local copies, waits for them, and re-layouts: 5.37 us -> 6.46 us
where the time goes in v2:
time: 114 us; the launch traced here: 113 us
  Pallas kernels  102 us (89%)
  local copies, waits for them, and re-layouts  6.47 us (6%)
  other arithmetic  3.68 us (3%)
    pallas_call x1, Pallas kernels, shards(): pl.pallas_call(kernel, out_shape=(shape((tokens, C), BF), shape((tokens,...  102 us
    unnamed x18, local copies, waits for them, and re-layouts  6.46 us
    convert_element_type x1, other arithmetic, shards(): grad_fields = (grad.astype(F32) + go.astype(F32)).astype(BF)  3.02 us

profile of v2, /device:TPU:0, one launch (start us, length us, event | category | flops | bytes accessed | tf_op | source)
XLA Modules:
  0.0 112.5 jit_solution(947555046082513267)
XLA Ops:
  0.6 0.7 add_convert_fusion.2
  1.3 0.0 copy-start
  1.3 1.0 copy-done
  2.3 0.0 copy-start.1
  2.3 1.0 copy-done.1
  3.3 0.0 copy-start.2
  3.3 0.9 copy-done.2
  4.2 0.0 copy-start.3
  4.2 0.9 copy-done.3
  5.1 0.0 copy-start.4
  5.1 0.7 copy-done.4
  5.9 0.0 copy-start.5
  5.9 0.7 copy-done.5
  6.5 0.0 copy-start.6
  6.6 0.0 copy-start.7
  6.6 101.7 %block.1 = (bf16[1728,512]{1,0:T(8,128)(2,1)S(1)}, bf16[1728,512]{1,0:T(8,128)(2,1)S(1)}, f32[12,512]{1,0:T(8,128)S(1)}, f32[4,512]{1,0:T(4,128)S(1)}) custom-call(bf16[1728,512]{1,0:T(8,128)(2,1)} %bitcast.14, bf16[1728,512]{1,0:T(8,128)(2,1)} %bitcast.15, f32[8,128]{1,0:T(8,128)S(1)} %broadcast_in_dim.2.reg_ref, bf16[12,512]{1,0:T(8,128)(2,1)S(1)} %copy-done.4, ...), custom_call_target="tpu_custom_call" | custom-call | tf_op jit(solution)/shard_map/block/pallas_call | solution.py:464
  108.3 0.0 copy-done.6
  108.3 0.0 copy-done.7
  108.3 3.0 %add_convert_fusion = (bf16[1728,512]{1,0:T(8,128)(2,1)}, bf16[1728,512]{1,0:T(8,128)(2,1)}) fusion(bf16[1728,512]{1,0:T(8,128)(2,1)S(1)} %get-tuple-element.9, bf16[24,24,3,512]{3,1,2,0:T(8,128)(2,1)S(1)} %copy-done.7, bf16[1728,512]{1,0:T(8,128)(2,1)S(1)} %get-tuple-element.8, bf16[24,24,3,512]{3,1,2,0:T(8,128)(2,1)S(1)} %copy-done.6), kind=kLoop, calls=%fused_computation | loop fusion | flops 7077888 | bytes 10616832 | tf_op jit(solution)/shard_map/convert_element_type | solution.py:515
  111.3 0.6 copy.15
  111.9 0.6 copy.16
  (2 shorter events, 0.0 us)
Async XLA Ops:
  1.3 1.0 copy-start
  2.3 1.0 copy-start.1
  3.3 0.9 copy-start.2
  4.2 0.9 copy-start.3
  5.1 0.7 copy-start.4
  5.9 0.7 copy-start.5
  6.5 101.7 %copy-start.6 = (bf16[24,24,3,512]{3,1,2,0:T(8,128)(2,1)S(1)}, bf16[24,24,3,512]{3,1,2,0:T(8,128)(2,1)}, u32[]{:S(2)}) copy-start(bf16[24,24,3,512]{3,1,2,0:T(8,128)(2,1)} %param.9) | copy-start | bytes 5308420
  6.6 101.7 %copy-start.7 = (bf16[24,24,3,512]{3,1,2,0:T(8,128)(2,1)S(1)}, bf16[24,24,3,512]{3,1,2,0:T(8,128)(2,1)}, u32[]{:S(2)}) copy-start(bf16[24,24,3,512]{3,1,2,0:T(8,128)(2,1)} %param.13) | copy-start | bytes 5308420

commit v3 on v2

--- a/solution.py
+++ b/solution.py
@@ -12,7 +12,7 @@
 SLOT = 112
 N = 4 * SLOT
 C = 512
-BLK = 112
+BLK = 224
 FACTOR = float(221184) ** (-0.5)
 MESH = pl.DeviceIdType.MESH
 AG_ORDER = (("z", "x", "y"), ("z", "y", "x"), ("z", "x", "y"), ("z", "y", "x"))
@@ -99,49 +99,67 @@
     return centre * inverse, inverse
 
 
-def window(w, half, which, xg, reg_s, wq, wp, ow, normed_s, att_s, gqkv_s, qkv_s, ga_s, bias_s, r_s, t_s):
-    normal, inverse = normalised(xg[0, w].reshape(N, C))
-    normed = normal.astype(BF)
-    normed_s[w] = normed
-    col, row = token_regions(reg_s[which, 0:1, :], half)
-    bias_s[...] = jnp.where(col == row, 0.0, -1e30)
+def mask_of(reg_row, half, bias):
+    col, row = token_regions(reg_row, half)
+    bias[...] = jnp.where(col == row, 0.0, -1e30)
+
+
+def window(w, xg, wq, wp, ow, normed_s, att_s, gqkv_s, qkv_s, ga_s, bias, r_s, t_s):
+    normed = normed_s[w]
     qkv_s[:, :512] = nt(normed, wq[0:512, :]).astype(BF) * jnp.asarray(0.125, BF)
     qkv_s[:, 512:1024] = nt(normed, wq[512:1024, :]).astype(BF)
     qkv_s[:, 1024:] = nt(normed, wq[1024:, :]).astype(BF)
     ga_s[...] = nn(xg[1, w].reshape(N, C), wp[...]).astype(BF)
     low = lax.broadcasted_iota(jnp.int32, (N, 128), 1) < 64
 
-    def pair(hp, _):
-        o = pl.multiple_of(hp * 128, 128)
-        q2 = qkv_s[:, pl.ds(o, 128)]
-        k2 = qkv_s[:, pl.ds(512 + o, 128)]
-        v2 = qkv_s[:, pl.ds(1024 + o, 128)]
-        g2 = ga_s[:, pl.ds(o, 128)]
-        outs = []
-        for h in range(2):
-            keep = low if h == 0 else jnp.logical_not(low)
-            qa = jnp.where(keep, q2, jnp.zeros_like(q2))
-            gaa = jnp.where(keep, g2, jnp.zeros_like(g2))
-            for b in range(0, N, BLK):
-                s = nt(qa[b : b + BLK], k2) + bias_s[b : b + BLK, :]
-                m = jnp.max(s, axis=-1, keepdims=True)
-                e = jnp.exp(s - m)
-                p = e * (1.0 / jnp.sum(e, axis=-1, keepdims=True))
-                r_s[h, b : b + BLK, :] = p.astype(BF)
-                dp = nt(gaa[b : b + BLK], v2)
-                inner = jnp.sum(dp * p, axis=-1, keepdims=True)
-                t_s[h, b : b + BLK, :] = (p * (dp - inner)).astype(BF)
-            r = r_s[h]
-            t = t_s[h]
-            outs.append((nn(r, v2), nn(t, k2), tn(t, q2), tn(r, g2)))
-        att, dq, dk, dv = [jnp.where(low, a, b) for a, b in zip(*outs)]
-        att_s[w, :, pl.ds(o, 128)] = att.astype(BF)
-        gqkv_s[w, :, pl.ds(o, 128)] = (dq * 0.125).astype(BF)
-        gqkv_s[w, :, pl.ds(512 + o, 128)] = dk.astype(BF)
-        gqkv_s[w, :, pl.ds(1024 + o, 128)] = dv.astype(BF)
-        return 0
-
-    lax.fori_loop(0, 4, pair, 0)
+    def pair(ref, base, head):
+        o = base + 128 * (head // 2)
+        return ref[:, o : o + 128]
+
+    def alone(v, head):
+        return jnp.where(low if head % 2 == 0 else jnp.logical_not(low), v, jnp.zeros_like(v))
+
+    def weigh(head, b):
+        query = alone(pair(qkv_s, 0, head), head)[b : b + BLK]
+        grad = alone(pair(ga_s, 0, head), head)[b : b + BLK]
+        s = nt(query, pair(qkv_s, 512, head))
+        dp = nt(grad, pair(qkv_s, 1024, head))
+        s = s + bias[b : b + BLK, :]
+        m = jnp.max(s, axis=-1, keepdims=True)
+        e = jnp.exp(s - m)
+        p = e * (1.0 / jnp.sum(e, axis=-1, keepdims=True))
+        r_s[head % 2, b : b + BLK, :] = p.astype(BF)
+        inner = jnp.sum(dp * p, axis=-1, keepdims=True)
+        t_s[head % 2, b : b + BLK, :] = (p * (dp - inner)).astype(BF)
+
+    sums = {}
+
+    def mix(head, part):
+        r, t = r_s.at[head % 2], t_s.at[head % 2]
+        if part == 0:
+            sums[head, 0] = nn(r[...], pair(qkv_s, 1024, head))
+            sums[head, 1] = nn(t[...], pair(qkv_s, 512, head))
+        else:
+            sums[head, 2] = tn(t[...], pair(qkv_s, 0, head))
+            sums[head, 3] = tn(r[...], pair(ga_s, 0, head))
+        if head % 2 == 1:
+            o = 128 * (head // 2)
+            for i in (2 * part, 2 * part + 1):
+                v = jnp.where(low, sums.pop((head - 1, i)), sums.pop((head, i)))
+                if i == 0:
+                    att_s[w, :, o : o + 128] = v.astype(BF)
+                else:
+                    v = v * 0.125 if i == 1 else v
+                    at = 512 * (i - 1) + o
+                    gqkv_s[w, :, at : at + 128] = v.astype(BF)
+
+    for head in range(9):
+        for n in range(2):
+            if head < 8:
+                weigh(head, n * BLK)
+            if head > 0:
+                mix(head - 1, n)
+
     ow[0, w] = nt(att_s[w], wp[...]).astype(BF).reshape(4, SLOT, C)
     grad = nn(gqkv_s[w], wq[...])
     normal, inverse = normalised(xg[0, w].reshape(N, C))
@@ -154,9 +172,9 @@
 
 
 def kernel(
-    f_hbm, g_hbm, reg_ref, wq_ref, wp_ref, cut_hbm, paste_hbm, pick_hbm, pack_hbm,
+    f_hbm, g_hbm, reg_hbm, wq_hbm, wp_hbm, cut_hbm, paste_hbm, pick_hbm, pack_hbm,
     fo_ref, go_ref, qo_ref, po_ref,
-    f_ref, g_ref, cut_ref, paste_ref, pick_ref, pack_ref, load_sem,
+    f_ref, g_ref, cut_ref, paste_ref, pick_ref, pack_ref, wq_ref, wp_ref, reg_ref, load_sem,
     own_s, wg, wq, wp, stage, xg, reg_s, ow, rq,
     normed_s, att_s, gqkv_s, qkv_s, ga_s, bias_s, r_s, t_s,
     gw_s, pk, rc, h0, rb0, h1, rb1, h2, rb2,
@@ -182,31 +200,33 @@
             (
                 (f_hbm, f_ref), (g_hbm, g_ref), (cut_hbm, cut_ref),
                 (pick_hbm, pick_ref), (paste_hbm, paste_ref), (pack_hbm, pack_ref),
+                (wq_hbm, wq_ref), (wp_hbm, wp_ref), (reg_hbm, reg_ref),
             )
         )
     ]
-    for c in loads:
+    for c in loads[6:] + loads[:6]:
         c.start()
 
+    loads[6].wait()
+    loads[7].wait()
     own_s[0:12, :] = wq_ref[...].astype(F32)
     own_s[12:16, :] = wp_ref[...].astype(F32)
     for k in range(4):
-        wg[k, me.zlo, me.x, me.core, me.y, me.zhi] = own_s[:, 128 * k : 128 * k + 128].astype(BF)
-    reg_s[0] = reg_ref[...]
+        outer, inner = (getattr(me, d) for d in AG_ORDER[k][:0:-1])
+        wg[k, me.core, outer, inner, me.z] = own_s[:, 128 * k : 128 * k + 128].astype(BF)
+    loads[8].wait()
+    lane = lax.broadcasted_iota(jnp.int32, (8, 128), 1)
+    regions = jnp.zeros((8, 128), jnp.int32)
+    for n in range(24):
+        regions = jnp.where(lane == n, reg_ref[n] + 1, regions)
+    reg_s[0] = regions.astype(F32)
     pl.semaphore_wait(barrier, len(greeted))
 
     every = slice(None)
 
     def held(k, done, **fixed):
-        z = fixed.get("z", me.z)
-        return wg.at[
-            k,
-            every if "z" in done else z % 2,
-            every if "x" in done else fixed.get("x", me.x),
-            me.core,
-            every if "y" in done else fixed.get("y", me.y),
-            every if "z" in done else z // 2,
-        ]
+        own = (every if d in done else fixed.get(d, getattr(me, d)) for d in AG_ORDER[k][::-1])
+        return wg.at[(k, me.core, *own)]
 
     gathers = []
     forwards = []
@@ -268,25 +288,36 @@
     cut(1, (("out", 5), ("own", 0, 0), ("own", 0, 1), ("own", 1, 0)))
     gather_step(1)
     cut(2, (("out", 6), ("own", 0, 2), ("own", 0, 3), ("own", 1, 2)))
+    normed_s[0] = normalised(xg[0, 0].reshape(N, C))[0].astype(BF)
     gather_step(2)
+    mask_of(reg_s[0, 0:1, :], 0, bias_s.at[0])
+    mask_of(reg_s[0, 0:1, :], 1, bias_s.at[1])
     cut(0, (("own", 3, 3), ("out", 0), ("out", 1), ("out", 2)))
+    send_in("s", 0, 2, 2, 2, me.beside(0, -1), 0)
     cut(3, (("out", 3), ("own", 2, 0), ("own", 2, 1), ("out", 4)))
     gather_end()
     send_in("e", 5, 1, 1, 1, me.beside(-1, 0), 4)
     send_in("e", 6, 1, 3, 1, me.beside(-1, 0), 5)
-    send_in("s", 0, 2, 2, 2, me.beside(0, -1), 0)
     send_in("c", 2, 3, 2, 1, me.beside(1, 0), 1)
     c = copy(reg_s.at[0], reg_s.at[1], in_a.at[6], in_b.at[6], me.beside(0, 1))
     c.start()
     halos["c"].append(c)
     send_in("c", 3, 3, 1, 1, me.beside(0, 1), 2)
     send_in("c", 4, 3, 0, 1, me.beside(1, 1), 3)
-    for c in loads[3:]:
+    for c in loads[3:6]:
         c.wait()
+
+    inside = [(core, y, zhi) for core in range(2) for y in range(4) for zhi in range(2)]
+
+    def spot(k, j, core, y, zhi):
+        z = 2 * zhi + j // 4
+        return (k, core, y, j % 4, z) if AG_ORDER[k][2] == "y" else (k, core, j % 4, y, z)
 
     def unpack(j, _):
         for half in range(2):
-            parts = [wg[2 * half + k, j // 4, j % 4].reshape(256, 128) for k in range(2)]
+            parts = [
+                jnp.concatenate([wg[spot(k, j, *i)] for i in inside], axis=0) for k in (2 * half, 2 * half + 1)
+            ]
             got = nn(pick_ref[...], jnp.concatenate(parts, axis=1)).astype(BF)
             wq[pl.ds(pl.multiple_of(192 * j, 64), 192), 256 * half : 256 * half + 256] = got[:192]
             wp[pl.ds(pl.multiple_of(64 * j, 64), 64), 256 * half : 256 * half + 256] = got[192:]
@@ -317,7 +348,16 @@
                 for c in halos[name]:
                     c.wait_recv()
 
-        window(i, i // 2, i // 3, xg, reg_s, wq, wp, ow, normed_s, att_s, gqkv_s, qkv_s, ga_s, bias_s, r_s, t_s)
+        @pl.when(i > 0)
+        def _():
+            normed_s[i] = normalised(xg[0, i].reshape(N, C))[0].astype(BF)
+
+        @pl.when(i == 3)
+        def _():
+            mask_of(reg_s[1, 0:1, :], 1, bias_s.at[2])
+
+        bias = bias_s.at[jnp.maximum(i - 1, 0)]
+        window(i, xg, wq, wp, ow, normed_s, att_s, gqkv_s, qkv_s, ga_s, bias, r_s, t_s)
         for step in (1, 2, 3):
 
             @pl.when(i == step)
@@ -340,77 +380,53 @@
     lax.fori_loop(0, 6, weight_chunk, 0)
     gw_s[1536:2048, :] = (tn(xg[1].reshape(4 * N, C), att_s[...].reshape(4 * N, C)) * FACTOR).astype(BF)
 
-    def across(j):
-        return copy(
-            pk.at[:, j // 4, j % 4, 1 - me.core], rc.at[:, j // 4, j % 4], rc_a.at[j], rc_b.at[j], sibling
-        )
-
-    def pack(j, _):
-        rows = jnp.concatenate(
-            [
-                gw_s[pl.ds(pl.multiple_of(192 * j, 64), 192), :],
-                gw_s[pl.ds(pl.multiple_of(1536 + 64 * j, 64), 64), :],
-            ],
-            axis=0,
-        )
-        got = nn(pack_ref[...], rows).astype(BF)
-        for k in range(4):
-            pk[k, j // 4, j % 4] = got[:, 128 * k : 128 * k + 128].reshape(2, 4, 2, 16, 128)
-        across(j).start()
-        return 0
-
-    lax.fori_loop(0, 8, pack, 0)
-
-    def merge(j, _):
-        across(j).wait_recv()
-        mine = pk[:, j // 4, j % 4, me.core].astype(F32)
-        h0[:, j // 4, j % 4] = (mine + rc[:, j // 4, j % 4].astype(F32)).astype(BF)
-        return 0
-
-    lax.fori_loop(0, 8, merge, 0)
+    crossing = [copy(pk.at[k, 1 - me.core], rc.at[k], rc_a.at[k], rc_b.at[k], sibling) for k in range(4)]
+    for half in range(2):
+
+        def pack(j, _):
+            rows = jnp.concatenate(
+                [
+                    gw_s[pl.ds(pl.multiple_of(192 * j, 64), 192), 256 * half : 256 * half + 256],
+                    gw_s[pl.ds(pl.multiple_of(1536 + 64 * j, 64), 64), 256 * half : 256 * half + 256],
+                ],
+                axis=0,
+            )
+            got = nn(pack_ref[...], rows).astype(BF)
+            for n, i in enumerate(inside):
+                for k in range(2):
+                    pk[spot(2 * half + k, j, *i)] = got[16 * n : 16 * n + 16, 128 * k : 128 * k + 128]
+            return 0
+
+        lax.fori_loop(0, 8, pack, 0)
+        crossing[2 * half].start()
+        crossing[2 * half + 1].start()
 
     reduces = []
 
-    def reduce_step(stage_index):
-        for k in range(4):
-            order = RS_ORDER[k]
-            started = []
-            for step in (1, 2, 3):
-                there, device = me.along(order[stage_index], step)
-                if stage_index == 0:
-                    src = h0.at[k, :, :, there] if order[0] == "y" else h0.at[k, :, there]
-                    dst = rb0.at[k, step - 1]
-                elif stage_index == 1:
-                    src, dst = h1.at[k, :, there], rb1.at[k, step - 1]
-                else:
-                    src, dst = h2.at[k, there % 2, there // 2], rb2.at[k, step - 1]
-                sem = k * 9 + stage_index * 3 + step - 1
-                c = copy(src, dst, rs_a.at[sem], rs_b.at[sem], device)
-                c.start()
-                started.append(c)
-            reduces.append(started)
-
-    def reduce_take(stage_index):
-        for k in range(4):
-            order = RS_ORDER[k]
-            for c in reduces[4 * stage_index + k]:
-                c.wait_recv()
-            got = (rb0, rb1, rb2)[stage_index]
-            if stage_index == 0:
-                mine = h0[k, :, :, me.y] if order[0] == "y" else h0[k, :, me.x]
-            elif stage_index == 1:
-                mine = h1[k, :, getattr(me, order[1])]
-            else:
-                mine = h2[k, me.zlo, me.zhi]
-            total = mine.astype(F32)
-            for step in range(3):
-                total = total + got[k, step].astype(F32)
-            if stage_index == 0:
-                h1[k] = total.astype(BF)
-            elif stage_index == 1:
-                h2[k] = total.astype(BF)
-            else:
-                own_s[:, 128 * k : 128 * k + 128] = total
+    def reduce_step(stage_index, k):
+        order = RS_ORDER[k]
+        started = []
+        for step in (2, 1, 3):
+            there, device = me.along(order[stage_index], step)
+            src = (h0, h1, h2)[stage_index].at[k, there]
+            dst = (rb0, rb1, rb2)[stage_index].at[k, step - 1]
+            sem = k * 9 + stage_index * 3 + step - 1
+            c = copy(src, dst, rs_a.at[sem], rs_b.at[sem], device)
+            c.start()
+            started.append(c)
+        reduces.append(started)
+
+    def reduce_take(stage_index, k):
+        for c in reduces[4 * stage_index + k]:
+            c.wait_recv()
+        got = (rb0, rb1, rb2)[stage_index]
+        total = (h0, h1, h2)[stage_index][k, getattr(me, RS_ORDER[k][stage_index])].astype(F32)
+        for step in range(3):
+            total = total + got[k, step].astype(F32)
+        if stage_index < 2:
+            (h1, h2)[stage_index][k] = total.astype(BF)
+        else:
+            own_s[:, 128 * k : 128 * k + 128] = total
 
     mine = {
         (1, 1): (0, 0), (1, 2): (0, 1), (2, 1): (0, 2), (2, 2): (0, 3), (1, 3): (1, 0),
@@ -418,7 +434,7 @@
     }
 
     def paste(qi):
-        for a, out in ((0, fo_ref), (1, go_ref)):
+        for a, ref, out in ((0, f_ref, fo_ref), (1, g_ref, go_ref)):
             quarters = []
             for qj in range(4):
                 if (qi, qj) in mine:
@@ -426,45 +442,67 @@
                 else:
                     quarters.append(rq[a, qi, qj])
             back = nn(paste_ref[...], jnp.concatenate(quarters, axis=0))
-            out[432 * qi : 432 * qi + 432, :] = back.astype(BF)
-
-    reduce_step(0)
+            rows = slice(432 * qi, 432 * qi + 432)
+            out[rows, :] = (ref[rows, :].astype(F32) + back).astype(BF)
+
+    for k in range(4):
+        crossing[k].wait_recv()
+        h0[k] = (pk[k, me.core].astype(F32) + rc[k].astype(F32)).astype(BF)
+        reduce_step(0, k)
     for c in returns:
         c.wait_recv()
     paste(1)
     paste(2)
-    reduce_take(0)
-    reduce_step(1)
+    for k in range(4):
+        reduce_take(0, k)
+        reduce_step(1, k)
     paste(0)
-    reduce_take(1)
-    reduce_step(2)
+    for k in range(4):
+        reduce_take(1, k)
+        reduce_step(2, k)
     paste(3)
-    reduce_take(2)
+    for k in range(4):
+        reduce_take(2, k)
     qo_ref[...] = own_s[0:12, :]
     po_ref[...] = own_s[12:16, :]
 
-    for started in gathers + reduces + [returns, forwards] + list(halos.values()):
+    for started in gathers + reduces + [returns, forwards, crossing] + list(halos.values()):
         for c in started:
             c.wait_send()
-    for j in range(8):
-        across(j).wait_send()
+
+
+def settle(fo, go, qo, po, f_out, g_out, q_out, p_out, f_s, g_s, q_s, p_s, in_sem, out_sem):
+    parts = [(qo, q_s, q_out), (po, p_s, p_out)]
+    for n in range(0, 1728, 432):
+        rows = pl.ds(n, 432)
+        parts.append((fo.at[rows], f_s.at[rows], f_out.at[rows]))
+        parts.append((go.at[rows], g_s.at[rows], g_out.at[rows]))
+    inward = [pltpu.make_async_copy(a, b, in_sem.at[n]) for n, (a, b, c) in enumerate(parts)]
+    outward = [pltpu.make_async_copy(b, c, out_sem.at[n]) for n, (a, b, c) in enumerate(parts)]
+    for c in inward:
+        c.start()
+    for c, d in zip(inward, outward):
+        c.wait()
+        d.start()
+    for d in outward:
+        d.wait()
 
 
 def shards(fields, region_ids, w_qkv, w_proj, grad_output):
     tokens = 24 * 24 * 3
     flat = fields.transpose(0, 2, 1, 3).reshape(tokens, C)
     grad = grad_output.transpose(0, 2, 1, 3).reshape(tokens, C)
-    regions = jnp.broadcast_to(jnp.pad((region_ids + 1).astype(F32), (0, 104))[None], (8, 128))
     cut = cut_matrix()
     pick = unpack_matrix()
     vm = pl.BlockSpec(memory_space=pltpu.VMEM)
-    hbm = pl.BlockSpec(memory_space=pl.ANY)
+    hbm = pl.BlockSpec(memory_space=pltpu.HBM)
+    anywhere = pl.BlockSpec(memory_space=pl.ANY)
     shape = jax.ShapeDtypeStruct
     dma = pltpu.SemaphoreType.DMA
     fo, go, qo, po = pl.pallas_call(
         kernel,
         out_shape=(shape((tokens, C), BF), shape((tokens, C), BF), shape((12, C), F32), shape((4, C), F32)),
-        in_specs=[hbm] * 2 + [vm] * 3 + [hbm] * 4,
+        in_specs=[hbm] * 9,
         out_specs=[vm] * 4,
         scratch_shapes=[
             pltpu.VMEM((tokens, C), BF),
@@ -473,9 +511,12 @@
             pltpu.VMEM((432, N), BF),
             pltpu.VMEM((256, 256), BF),
             pltpu.VMEM((256, 256), BF),
-            dma((6,)),
+            pltpu.VMEM((12, C), BF),
+            pltpu.VMEM((4, C), BF),
+            pltpu.SMEM((24,), jnp.int32),
+            dma((9,)),
             pltpu.VMEM((16, C), F32),
-            pltpu.VMEM((4, 2, 4, 2, 4, 2, 16, 128), BF),
+            pltpu.VMEM((4, 2, 4, 4, 4, 16, 128), BF),
             pltpu.VMEM((1536, C), BF),
             pltpu.VMEM((C, C), BF),
             pltpu.VMEM((2, 7, SLOT, C), BF),
@@ -488,31 +529,45 @@
             pltpu.VMEM((4, N, 3 * C), BF),
             pltpu.VMEM((N, 3 * C), BF),
             pltpu.VMEM((N, C), BF),
-            pltpu.VMEM((N, N), F32),
+            pltpu.VMEM((3, N, N), F32),
             pltpu.VMEM((2, N, N), BF),
             pltpu.VMEM((2, N, N), BF),
             pltpu.VMEM((2048, C), BF),
-            pltpu.VMEM((4, 2, 4, 2, 4, 2, 16, 128), BF),
-            pltpu.VMEM((4, 2, 4, 4, 2, 16, 128), BF),
-            pltpu.VMEM((4, 2, 4, 4, 2, 16, 128), BF),
-            pltpu.VMEM((4, 3, 2, 4, 2, 16, 128), BF),
-            pltpu.VMEM((4, 2, 4, 2, 16, 128), BF),
-            pltpu.VMEM((4, 3, 2, 2, 16, 128), BF),
-            pltpu.VMEM((4, 2, 2, 16, 128), BF),
+            pltpu.VMEM((4, 2, 4, 4, 4, 16, 128), BF),
+            pltpu.VMEM((4, 4, 4, 4, 16, 128), BF),
+            pltpu.VMEM((4, 4, 4, 4, 16, 128), BF),
+            pltpu.VMEM((4, 3, 4, 4, 16, 128), BF),
+            pltpu.VMEM((4, 4, 4, 16, 128), BF),
+            pltpu.VMEM((4, 3, 4, 16, 128), BF),
+            pltpu.VMEM((4, 4, 16, 128), BF),
             pltpu.VMEM((4, 3, 16, 128), BF),
             dma((52,)), dma((52,)), dma((7,)), dma((7,)), dma((6,)), dma((6,)),
-            dma((8,)), dma((8,)), dma((36,)), dma((36,)),
+            dma((4,)), dma((4,)), dma((36,)), dma((36,)),
         ],
         compiler_params=pltpu.CompilerParams(
-            collective_id=0, has_side_effects=True, vmem_limit_bytes=48 * 1024 * 1024
+            collective_id=0, has_side_effects=True, vmem_limit_bytes=56 * 1024 * 1024
         ),
         name="block",
     )(
-        flat, grad, regions, w_qkv, w_proj,
+        flat, grad, region_ids, w_qkv, w_proj,
         jnp.asarray(cut, BF), jnp.asarray(cut.T, BF), jnp.asarray(pick, BF), jnp.asarray(pick.T, BF),
     )
-    block_out = (flat.astype(F32) + fo.astype(F32)).astype(BF)
-    grad_fields = (grad.astype(F32) + go.astype(F32)).astype(BF)
+    block_out, grad_fields, qo, po = pl.pallas_call(
+        settle,
+        out_shape=(shape((tokens, C), BF), shape((tokens, C), BF), shape((12, C), F32), shape((4, C), F32)),
+        in_specs=[anywhere] * 4,
+        out_specs=[anywhere] * 4,
+        scratch_shapes=[
+            pltpu.VMEM((tokens, C), BF),
+            pltpu.VMEM((tokens, C), BF),
+            pltpu.VMEM((12, C), F32),
+            pltpu.VMEM((4, C), F32),
+            dma((10,)),
+            dma((10,)),
+        ],
+        compiler_params=pltpu.CompilerParams(vmem_limit_bytes=56 * 1024 * 1024),
+        name="settle",
+    )(fo, go, qo, po)
     block_out = block_out.reshape(24, 3, 24, C).transpose(0, 2, 1, 3)
     grad_fields = grad_fields.reshape(24, 3, 24, C).transpose(0, 2, 1, 3)
     return block_out, grad_fields, qo, po

time: 114 us -> 97.4 us (0.85)
  local copies, waits for them, and re-layouts: 6.47 us -> 0 us
  Pallas kernels: 102 us -> 95.9 us
  other arithmetic: 3.68 us -> 0 us
    pallas_call x1, Pallas kernels: 102 us -> 92.8 us  [shards(): pl.pallas_call(kernel, out_shape=(shape((tokens, C), BF), shape((tokens,...]
    unnamed x18 -> x0, local copies, waits for them, and re-layouts: 6.46 us -> none
    convert_element_type x2 -> x0, other arithmetic: 3.68 us -> none  [the longest x1 3.02 us: shards(): grad_fields = (grad.astype(F32) + go.astype(F32)).astype(BF)]
    pallas_call x0 -> x1, Pallas kernels: none -> 3.05 us  [shards(): pl.pallas_call(settle, out_shape=(shape((tokens, C), BF), shape((tokens,...]
where the time goes in v3:
time: 97.4 us; the launch traced here: 96.7 us
  Pallas kernels  95.9 us (98%)
    pallas_call x1, Pallas kernels, shards(): pl.pallas_call(kernel, out_shape=(shape((tokens, C), BF), shape((tokens,...  92.8 us
    pallas_call x1, Pallas kernels, shards(): pl.pallas_call(settle, out_shape=(shape((tokens, C), BF), shape((tokens,...  3.05 us

profile of v3, /device:TPU:0, one launch (start us, length us, event | category | flops | bytes accessed | tf_op | source)
XLA Modules:
  0.0 96.7 jit_solution(14620920601100797505)
XLA Ops:
  0.6 92.8 %block.1 = (bf16[1728,512]{1,0:T(8,128)(2,1)}, bf16[1728,512]{1,0:T(8,128)(2,1)}, f32[12,512]{1,0:T(8,128)}, f32[4,512]{1,0:T(4,128)}) custom-call(bf16[1728,512]{1,0:T(8,128)(2,1)} %bitcast.12, bf16[1728,512]{1,0:T(8,128)(2,1)} %bitcast.13, s32[24]{0:T(128)} %reg_hbm.1, bf16[12,512]{1,0:T(8,128)(2,1)} %wq_hbm.1, bf16[4,512]{1,0:T(4,128)(2,1)} %wp_hbm.1, ...), custom_call_target="tpu_custom_call" | custom-call | tf_op jit(solution)/shard_map/block/pallas_call | solution.py:502
  93.5 3.1 %settle.1 = (bf16[1728,512]{1,0:T(8,128)(2,1)}, bf16[1728,512]{1,0:T(8,128)(2,1)}, f32[12,512]{1,0:T(8,128)}, f32[4,512]{1,0:T(4,128)}) custom-call(bf16[1728,512]{1,0:T(8,128)(2,1)} %get-tuple-element.12.fo, bf16[1728,512]{1,0:T(8,128)(2,1)} %get-tuple-element.13.go, f32[12,512]{1,0:T(8,128)} %get-tuple-element.14.qo, f32[4,512]{1,0:T(4,128)} %get-tuple-element.15.po), custom_call_target="tpu_custom_call" | custom-call | tf_op jit(solution)/shard_map/settle/pallas_call | solution.py:555

commit v4 on v3

--- a/solution.py
+++ b/solution.py
@@ -104,7 +104,7 @@
     bias[...] = jnp.where(col == row, 0.0, -1e30)
 
 
-def window(w, xg, wq, wp, ow, normed_s, att_s, gqkv_s, qkv_s, ga_s, bias, r_s, t_s):
+def window(w, xg, wq, wp, normed_s, att_s, gqkv_s, qkv_s, ga_s, bias, r_s, t_s):
     normed = normed_s[w]
     qkv_s[:, :512] = nt(normed, wq[0:512, :]).astype(BF) * jnp.asarray(0.125, BF)
     qkv_s[:, 512:1024] = nt(normed, wq[512:1024, :]).astype(BF)
@@ -160,6 +160,8 @@
             if head > 0:
                 mix(head - 1, n)
 
+
+def finish(w, xg, wq, wp, ow, att_s, gqkv_s):
     ow[0, w] = nt(att_s[w], wp[...]).astype(BF).reshape(4, SLOT, C)
     grad = nn(gqkv_s[w], wq[...])
     normal, inverse = normalised(xg[0, w].reshape(N, C))
@@ -174,7 +176,7 @@
 def kernel(
     f_hbm, g_hbm, reg_hbm, wq_hbm, wp_hbm, cut_hbm, paste_hbm, pick_hbm, pack_hbm,
     fo_ref, go_ref, qo_ref, po_ref,
-    f_ref, g_ref, cut_ref, paste_ref, pick_ref, pack_ref, wq_ref, wp_ref, reg_ref, load_sem,
+    f_ref, g_ref, cut_ref, paste_ref, pick_ref, pack_ref, wq_ref, wp_ref, reg_ref, load_sem, store_sem,
     own_s, wg, wq, wp, stage, xg, reg_s, ow, rq,
     normed_s, att_s, gqkv_s, qkv_s, ga_s, bias_s, r_s, t_s,
     gw_s, pk, rc, h0, rb0, h1, rb1, h2, rb2,
@@ -254,13 +256,12 @@
                 forward(k, 0, part)
 
     def gather_end():
-        for n, step in enumerate((1, 3, 2)):
-            for k in range(4):
-                gathers[k - 4][n].wait_recv()
-                dim = AG_ORDER[k][2]
-                forward(k, step, held(k, AG_ORDER[k][:2], **{dim: me.along(dim, 4 - step)[0]}))
-        for c in forwards:
-            c.wait_recv()
+        for half in range(2):
+            for n, step in enumerate((1, 3, 2)):
+                for k in (2 * half, 2 * half + 1):
+                    gathers[k - 4][n].wait_recv()
+                    dim = AG_ORDER[k][2]
+                    forward(k, step, held(k, AG_ORDER[k][:2], **{dim: me.along(dim, 4 - step)[0]}))
 
     halos = {}
 
@@ -313,17 +314,21 @@
         z = 2 * zhi + j // 4
         return (k, core, y, j % 4, z) if AG_ORDER[k][2] == "y" else (k, core, j % 4, y, z)
 
-    def unpack(j, _):
-        for half in range(2):
+    for half in range(2):
+        mine_now = (forwards[2 * half : 2 * half + 2], forwards[4 + 6 * half : 10 + 6 * half])
+        for c in mine_now[0] + mine_now[1]:
+            c.wait_recv()
+
+        def unpack(j, _):
             parts = [
                 jnp.concatenate([wg[spot(k, j, *i)] for i in inside], axis=0) for k in (2 * half, 2 * half + 1)
             ]
             got = nn(pick_ref[...], jnp.concatenate(parts, axis=1)).astype(BF)
             wq[pl.ds(pl.multiple_of(192 * j, 64), 192), 256 * half : 256 * half + 256] = got[:192]
             wp[pl.ds(pl.multiple_of(64 * j, 64), 64), 256 * half : 256 * half + 256] = got[192:]
-        return 0
-
-    lax.fori_loop(0, 8, unpack, 0)
+            return 0
+
+        lax.fori_loop(0, 8, unpack, 0)
 
     def send_out(w, first, qi, qj, count, device, sem):
         return copy(
@@ -338,7 +343,7 @@
         send_out(1, 1, 1, 0, 1, me.beside(1, 0), 4),
         send_out(1, 3, 2, 0, 1, me.beside(1, 0), 5),
     ]
-    leaves = {1: (4, 5), 2: (0,), 3: (1, 2, 3)}
+    leaves = {1: (4, 5), 2: (0,), 3: (3, 2, 1)}
 
     def turn(i, _):
         for step, name in ((1, "e"), (2, "s"), (3, "c")):
@@ -357,7 +362,12 @@
             mask_of(reg_s[1, 0:1, :], 1, bias_s.at[2])
 
         bias = bias_s.at[jnp.maximum(i - 1, 0)]
-        window(i, xg, wq, wp, ow, normed_s, att_s, gqkv_s, qkv_s, ga_s, bias, r_s, t_s)
+        window(i, xg, wq, wp, normed_s, att_s, gqkv_s, qkv_s, ga_s, bias, r_s, t_s)
+
+        @pl.when(i > 0)
+        def _():
+            finish(i, xg, wq, wp, ow, att_s, gqkv_s)
+
         for step in (1, 2, 3):
 
             @pl.when(i == step)
@@ -369,19 +379,55 @@
 
     lax.fori_loop(0, 4, turn, 0)
 
-    normed = normed_s[...].reshape(4 * N, C)
-
-    def weight_chunk(i, _):
-        o = pl.multiple_of(i * 256, 256)
-        left = gqkv_s[:, :, pl.ds(o, 256)].reshape(4 * N, 256)
-        gw_s[pl.ds(o, 256), :] = (tn(left, normed) * FACTOR).astype(BF)
-        return 0
-
-    lax.fori_loop(0, 6, weight_chunk, 0)
-    gw_s[1536:2048, :] = (tn(xg[1].reshape(4 * N, C), att_s[...].reshape(4 * N, C)) * FACTOR).astype(BF)
-
     crossing = [copy(pk.at[k, 1 - me.core], rc.at[k], rc_a.at[k], rc_b.at[k], sibling) for k in range(4)]
+    reduces = []
+
+    def reduce_step(stage_index, k):
+        order = RS_ORDER[k]
+        started = []
+        for step in (2, 1, 3):
+            there, device = me.along(order[stage_index], step)
+            src = (h0, h1, h2)[stage_index].at[k, there]
+            dst = (rb0, rb1, rb2)[stage_index].at[k, step - 1]
+            sem = k * 9 + stage_index * 3 + step - 1
+            c = copy(src, dst, rs_a.at[sem], rs_b.at[sem], device)
+            c.start()
+            started.append(c)
+        reduces.append(started)
+
+    def reduce_take(stage_index, k):
+        for c in reduces[4 * stage_index + k]:
+            c.wait_recv()
+        got = (rb0, rb1, rb2)[stage_index]
+        total = (h0, h1, h2)[stage_index][k, getattr(me, RS_ORDER[k][stage_index])].astype(F32)
+        for step in range(3):
+            total = total + got[k, step].astype(F32)
+        if stage_index < 2:
+            (h1, h2)[stage_index][k] = total.astype(BF)
+        else:
+            own_s[:, 128 * k : 128 * k + 128] = total
+
+    def merge(k):
+        crossing[k].wait_recv()
+        h0[k] = (pk[k, me.core].astype(F32) + rc[k].astype(F32)).astype(BF)
+        reduce_step(0, k)
+
     for half in range(2):
+        cols = slice(256 * half, 256 * half + 256)
+        normed = normed_s[:, :, cols].reshape(4 * N, 256)
+
+        def weight_chunk(i, _):
+            o = pl.multiple_of(i * 256, 256)
+            left = gqkv_s[:, :, pl.ds(o, 256)].reshape(4 * N, 256)
+            gw_s[pl.ds(o, 256), cols] = (tn(left, normed) * FACTOR).astype(BF)
+            return 0
+
+        lax.fori_loop(0, 6, weight_chunk, 0)
+        right = att_s[:, :, cols].reshape(4 * N, 256)
+        gw_s[1536:2048, cols] = (tn(xg[1].reshape(4 * N, C), right) * FACTOR).astype(BF)
+        if half == 1:
+            merge(0)
+            merge(1)
 
         def pack(j, _):
             rows = jnp.concatenate(
@@ -401,37 +447,12 @@
         crossing[2 * half].start()
         crossing[2 * half + 1].start()
 
-    reduces = []
-
-    def reduce_step(stage_index, k):
-        order = RS_ORDER[k]
-        started = []
-        for step in (2, 1, 3):
-            there, device = me.along(order[stage_index], step)
-            src = (h0, h1, h2)[stage_index].at[k, there]
-            dst = (rb0, rb1, rb2)[stage_index].at[k, step - 1]
-            sem = k * 9 + stage_index * 3 + step - 1
-            c = copy(src, dst, rs_a.at[sem], rs_b.at[sem], device)
-            c.start()
-            started.append(c)
-        reduces.append(started)
-
-    def reduce_take(stage_index, k):
-        for c in reduces[4 * stage_index + k]:
-            c.wait_recv()
-        got = (rb0, rb1, rb2)[stage_index]
-        total = (h0, h1, h2)[stage_index][k, getattr(me, RS_ORDER[k][stage_index])].astype(F32)
-        for step in range(3):
-            total = total + got[k, step].astype(F32)
-        if stage_index < 2:
-            (h1, h2)[stage_index][k] = total.astype(BF)
-        else:
-            own_s[:, 128 * k : 128 * k + 128] = total
-
     mine = {
         (1, 1): (0, 0), (1, 2): (0, 1), (2, 1): (0, 2), (2, 2): (0, 3), (1, 3): (1, 0),
         (2, 3): (1, 2), (3, 1): (2, 0), (3, 2): (2, 1), (0, 0): (3, 3),
     }
+
+    stores = []
 
     def paste(qi):
         for a, ref, out in ((0, f_ref, fo_ref), (1, g_ref, go_ref)):
@@ -443,19 +464,23 @@
                     quarters.append(rq[a, qi, qj])
             back = nn(paste_ref[...], jnp.concatenate(quarters, axis=0))
             rows = slice(432 * qi, 432 * qi + 432)
-            out[rows, :] = (ref[rows, :].astype(F32) + back).astype(BF)
-
-    for k in range(4):
-        crossing[k].wait_recv()
-        h0[k] = (pk[k, me.core].astype(F32) + rc[k].astype(F32)).astype(BF)
-        reduce_step(0, k)
-    for c in returns:
-        c.wait_recv()
+            ref[rows, :] = (ref[rows, :].astype(F32) + back).astype(BF)
+            c = pltpu.make_async_copy(ref.at[rows], out.at[rows], store_sem.at[2 * qi + a])
+            c.start()
+            stores.append(c)
+
+    merge(2)
+    merge(3)
+    finish(0, xg, wq, wp, ow, att_s, gqkv_s)
+    for n in (4, 5):
+        returns[n].wait_recv()
     paste(1)
     paste(2)
     for k in range(4):
         reduce_take(0, k)
         reduce_step(1, k)
+    for n in range(4):
+        returns[n].wait_recv()
     paste(0)
     for k in range(4):
         reduce_take(1, k)
@@ -463,6 +488,8 @@
     paste(3)
     for k in range(4):
         reduce_take(2, k)
+    for c in stores:
+        c.wait()
     qo_ref[...] = own_s[0:12, :]
     po_ref[...] = own_s[12:16, :]
 
@@ -503,7 +530,7 @@
         kernel,
         out_shape=(shape((tokens, C), BF), shape((tokens, C), BF), shape((12, C), F32), shape((4, C), F32)),
         in_specs=[hbm] * 9,
-        out_specs=[vm] * 4,
+        out_specs=[anywhere] * 2 + [vm] * 2,
         scratch_shapes=[
             pltpu.VMEM((tokens, C), BF),
             pltpu.VMEM((tokens, C), BF),
@@ -515,6 +542,7 @@
             pltpu.VMEM((4, C), BF),
             pltpu.SMEM((24,), jnp.int32),
             dma((9,)),
+            dma((8,)),
             pltpu.VMEM((16, C), F32),
             pltpu.VMEM((4, 2, 4, 4, 4, 16, 128), BF),
             pltpu.VMEM((1536, C), BF),

time: 97.4 us -> 96.8 us (level)
  no operation moved by 1% of the time
where the time goes in v4:
time: 96.8 us; the launch traced here: 96.7 us
  Pallas kernels  95.9 us (99%)
    pallas_call x1, Pallas kernels, shards(): pl.pallas_call(kernel, out_shape=(shape((tokens, C), BF), shape((tokens,...  92.8 us
    pallas_call x1, Pallas kernels, shards(): pl.pallas_call(settle, out_shape=(shape((tokens, C), BF), shape((tokens,...  3.05 us

profile of v4, /device:TPU:0, one launch (start us, length us, event | category | flops | bytes accessed | tf_op | source)
XLA Modules:
  0.0 96.7 jit_solution(1797119509627402831)
XLA Ops:
  0.6 92.8 %block.1 = (bf16[1728,512]{1,0:T(8,128)(2,1)}, bf16[1728,512]{1,0:T(8,128)(2,1)}, f32[12,512]{1,0:T(8,128)}, f32[4,512]{1,0:T(4,128)}) custom-call(bf16[1728,512]{1,0:T(8,128)(2,1)} %bitcast.12, bf16[1728,512]{1,0:T(8,128)(2,1)} %bitcast.13, s32[24]{0:T(128)} %reg_hbm.1, bf16[12,512]{1,0:T(8,128)(2,1)} %wq_hbm.1, bf16[4,512]{1,0:T(4,128)(2,1)} %wp_hbm.1, ...), custom_call_target="tpu_custom_call" | custom-call | tf_op jit(solution)/shard_map/block/pallas_call | solution.py:529
  93.4 3.1 %settle.1 = (bf16[1728,512]{1,0:T(8,128)(2,1)}, bf16[1728,512]{1,0:T(8,128)(2,1)}, f32[12,512]{1,0:T(8,128)}, f32[4,512]{1,0:T(4,128)}) custom-call(bf16[1728,512]{1,0:T(8,128)(2,1)} %get-tuple-element.12.fo, bf16[1728,512]{1,0:T(8,128)(2,1)} %get-tuple-element.13.go, f32[12,512]{1,0:T(8,128)} %get-tuple-element.14.qo, f32[4,512]{1,0:T(4,128)} %get-tuple-element.15.po), custom_call_target="tpu_custom_call" | custom-call | tf_op jit(solution)/shard_map/settle/pallas_call | solution.py:583

commit v5 on v4

--- a/solution.py
+++ b/solution.py
@@ -216,12 +216,6 @@
     for k in range(4):
         outer, inner = (getattr(me, d) for d in AG_ORDER[k][:0:-1])
         wg[k, me.core, outer, inner, me.z] = own_s[:, 128 * k : 128 * k + 128].astype(BF)
-    loads[8].wait()
-    lane = lax.broadcasted_iota(jnp.int32, (8, 128), 1)
-    regions = jnp.zeros((8, 128), jnp.int32)
-    for n in range(24):
-        regions = jnp.where(lane == n, reg_ref[n] + 1, regions)
-    reg_s[0] = regions.astype(F32)
     pl.semaphore_wait(barrier, len(greeted))
 
     every = slice(None)
@@ -284,6 +278,12 @@
         halos.setdefault(name, []).append(c)
 
     gather_step(0)
+    loads[8].wait()
+    lane = lax.broadcasted_iota(jnp.int32, (8, 128), 1)
+    regions = jnp.zeros((8, 128), jnp.int32)
+    for n in range(24):
+        regions = jnp.where(lane == n, reg_ref[n] + 1, regions)
+    reg_s[0] = regions.astype(F32)
     for c in loads[:3]:
         c.wait()
     cut(1, (("out", 5), ("own", 0, 0), ("own", 0, 1), ("own", 1, 0)))

time: 96.8 us -> 96.8 us (level)
  no operation moved by 1% of the time
where the time goes in v5:
time: 96.8 us; the launch traced here: 96.7 us
  Pallas kernels  95.9 us (99%)
    pallas_call x1, Pallas kernels, shards(): pl.pallas_call(kernel, out_shape=(shape((tokens, C), BF), shape((tokens,...  92.8 us
    pallas_call x1, Pallas kernels, shards(): pl.pallas_call(settle, out_shape=(shape((tokens, C), BF), shape((tokens,...  3.05 us

profile of v5, /device:TPU:0, one launch (start us, length us, event | category | flops | bytes accessed | tf_op | source)
XLA Modules:
  0.0 96.7 jit_solution(1866483084637972778)
XLA Ops:
  0.6 92.8 %block.1 = (bf16[1728,512]{1,0:T(8,128)(2,1)}, bf16[1728,512]{1,0:T(8,128)(2,1)}, f32[12,512]{1,0:T(8,128)}, f32[4,512]{1,0:T(4,128)}) custom-call(bf16[1728,512]{1,0:T(8,128)(2,1)} %bitcast.12, bf16[1728,512]{1,0:T(8,128)(2,1)} %bitcast.13, s32[24]{0:T(128)} %reg_hbm.1, bf16[12,512]{1,0:T(8,128)(2,1)} %wq_hbm.1, bf16[4,512]{1,0:T(4,128)(2,1)} %wp_hbm.1, ...), custom_call_target="tpu_custom_call" | custom-call | tf_op jit(solution)/shard_map/block/pallas_call | solution.py:529
  93.4 3.1 %settle.1 = (bf16[1728,512]{1,0:T(8,128)(2,1)}, bf16[1728,512]{1,0:T(8,128)(2,1)}, f32[12,512]{1,0:T(8,128)}, f32[4,512]{1,0:T(4,128)}) custom-call(bf16[1728,512]{1,0:T(8,128)(2,1)} %get-tuple-element.12.fo, bf16[1728,512]{1,0:T(8,128)(2,1)} %get-tuple-element.13.go, f32[12,512]{1,0:T(8,128)} %get-tuple-element.14.qo, f32[4,512]{1,0:T(4,128)} %get-tuple-element.15.po), custom_call_target="tpu_custom_call" | custom-call | tf_op jit(solution)/shard_map/settle/pallas_call | solution.py:583
